TPU v7x, 32 devices: a whole 2x2x4 slice. The times are simulated.
32 devices in a mesh: patch: 2 (over y), exp: 4 (over z), tile: 2 (over x), band: 2 (over core).
Axes of the slice: x: 2, y: 2, z: 4, core: 2. Of those that a mesh axis runs over, the one named last changes fastest.
Arguments:
- images: bfloat16 [4, 2, 64, 128, 128], P(('patch', 'band'), 'tile', 'exp'), parts along dimension 0, may hold values from -6 to 6
- mask_bits: int32 [4, 2, 64, 128, 128], P(('patch', 'band'), 'tile', 'exp'), parts along dimension 0, may hold values from 0 to 7
- inv_var: float32 [4, 2, 64], P(('patch', 'band'), 'tile', 'exp'), parts along dimension 0, may hold values from 0.5 to 4
- routes: int32 [4, 2, 64, 1], P(('patch', 'band'), 'tile', 'exp'), parts along dimension 0, may hold values from 0 to 3; in each aligned block of 16 rows (0 to 15, 16 to 31, ..., all dimensions but the last counted through in order) at most 8 rows name the same one
- block_slot: int32 [4, 2, 64], P(('patch', 'band'), 'tile', 'exp'), parts along dimension 0, may hold values from 0 to 7
- kernel_index: int32 [4, 2, 64], P(('patch', 'band'), 'tile', 'exp'), parts along dimension 0, may hold values from 0 to 63
- coefficients: float32 [64, 3], replicated, may hold values from -4 to 4
Outputs:
- coadd: float32 [4, 512, 2048], P(('patch', 'band'), 'tile', 'exp'), parts along dimension 0
- detection: float32 [1024, 2048], P(('patch', 'tile'), 'exp'), parts along dimension 0
There are 2 independent parts, one for each index of `patch`. A program takes and returns all parts, laid end to end along the dimension named above; an argument that names none is the same for every part. Nothing has to cross between parts.
Inputs may be any that keep to these rules, and one draw needn't show every extreme that they name: Among the 16 sub-blocks of one device for one band and strip (an aligned block of routes), no tile column is named more than 8 times, and some tile column is named exactly 8 times.
All inputs are finite; a program needn't handle non-finite values.
Results may differ from a plain program's by a relative error of at most 0.0039.
Values may be sent and summed in bfloat16 or wider, within the bound.
No kernel may reach another device: no remote copies, remote signals or barrier semaphores. Data moves between devices by JAX's collectives and lax.ppermute only.
A program may use at most 128 MiB of HBM per device.

v0:
```python
import jax
import jax.numpy as jnp
from jax import lax
from jax.sharding import PartitionSpec as P

BLOCK = 128
TAPS = 41
BLOCK_ROWS = 2
BLOCK_COLS = 4


kernel_sigmas = (1.0, 2.5, 6.0)


def extended(block, sides, width):
    for axis, dim in sides:
        count = lax.axis_size(axis)
        forward = [(i, i + 1) for i in range(count - 1)]
        backward = [(target, source) for source, target in forward]
        low = lax.ppermute(
            lax.slice_in_dim(block, block.shape[dim] - width, None, axis=dim), axis, forward
        )
        high = lax.ppermute(lax.slice_in_dim(block, 0, width, axis=dim), axis, backward)
        block = jnp.concatenate([low, block, high], axis=dim)
    return block


def usable_share(bits):
    flagged = jnp.bitwise_and(bits, 6) == 6
    suspect = jnp.bitwise_and(bits, 1).astype(jnp.float32)
    return jnp.where(flagged, 0.0, 1.0 - 0.5 * suspect)


def band_matrix(length, half_span):
    rows_here = jnp.arange(length + 2 * half_span, dtype=jnp.int32)[:, None]
    cols_here = jnp.arange(length, dtype=jnp.int32)[None, :]
    offset = (rows_here - cols_here - half_span).astype(jnp.float32)
    inside = jnp.abs(offset) <= half_span
    taps_axis = jnp.arange(-half_span, half_span + 1).astype(jnp.float32)
    result = []
    for spread in kernel_sigmas:
        norm_sum = jnp.sum(jnp.exp(-taps_axis * taps_axis / (2.0 * spread * spread)))
        result.append(
            jnp.where(inside, jnp.exp(-offset * offset / (2.0 * spread * spread)), 0.0) / norm_sum
        )
    return jnp.stack(result)


def local(images, mask_bits, inv_var, routes, block_slot, kernel_index, coefficients):
    peer_count = lax.axis_size("exp")
    held_count = images.shape[2]
    capacity = max(2, 2 * held_count // peer_count)
    slot_count = peer_count * capacity
    pixels = BLOCK * BLOCK
    tile_blocks = BLOCK_ROWS * BLOCK_COLS
    coef_count = coefficients.shape[0]
    usable = usable_share(mask_bits[0, 0])
    inverse = inv_var[0, 0][:, None, None]
    weight = (usable * inverse).astype(jnp.bfloat16).reshape(held_count, pixels)
    weighted = (
        (usable * inverse * images[0, 0].astype(jnp.float32))
        .astype(jnp.bfloat16)
        .reshape(held_count, pixels)
    )
    target = routes[0, 0, :, 0]
    ordinal = jnp.arange(held_count, dtype=jnp.int32)
    same_target = target[:, None] == target[None, :]
    earlier = jnp.sum(
        (same_target & (ordinal[None, :] < ordinal[:, None])).astype(jnp.int32), axis=1
    )
    position = target * capacity + earlier
    placed = jnp.arange(slot_count, dtype=jnp.int32)[:, None] == position[None, :]
    placed_int = placed.astype(jnp.int32)
    slot_block = jnp.sum(placed_int * (block_slot[0, 0] + 1)[None, :], axis=1) - 1
    slot_kernel = jnp.sum(placed_int * kernel_index[0, 0][None, :], axis=1)
    labels = jnp.stack([slot_block, slot_kernel], axis=1).reshape(peer_count, capacity, 2)
    placed_half = placed.astype(jnp.bfloat16)
    send_weight = (
        jnp.dot(placed_half, weight, preferred_element_type=jnp.float32)
        .astype(jnp.bfloat16)
        .reshape(peer_count, capacity, pixels)
    )
    block_ids = jnp.arange(tile_blocks, dtype=jnp.int32)[:, None]
    send_weighted = (
        jnp.dot(placed_half, weighted, preferred_element_type=jnp.float32)
        .astype(jnp.bfloat16)
        .reshape(peer_count, capacity, pixels)
    )
    got_weighted, got_weight, got_labels = (
        lax.all_to_all(send_weighted, "exp", split_axis=0, concat_axis=0, tiled=True),
        lax.all_to_all(send_weight, "exp", split_axis=0, concat_axis=0, tiled=True),
        lax.all_to_all(labels, "exp", split_axis=0, concat_axis=0, tiled=True),
    )
    got_labels = got_labels.reshape(slot_count, 2)
    into_block = block_ids == got_labels[:, 0][None, :]
    kernel_pick = (
        got_labels[:, 1][:, None] == jnp.arange(coef_count, dtype=jnp.int32)[None, :]
    ).astype(jnp.float32)
    slot_mix = jnp.dot(kernel_pick, coefficients, precision=lax.Precision.HIGHEST)
    mixing = slot_mix.T[:, None, :] * into_block.astype(jnp.float32)[None, :, :]
    basis_sum = jnp.einsum(
        "kbp,px->kbx",
        mixing,
        got_weighted.reshape(slot_count, pixels).astype(jnp.float32),
        precision=lax.Precision.HIGHEST,
    )
    depth_sum = jnp.dot(
        into_block.astype(jnp.bfloat16),
        got_weight.reshape(slot_count, pixels),
        preferred_element_type=jnp.float32,
    )
    tile_rows = BLOCK_ROWS * BLOCK
    tile_cols = BLOCK_COLS * BLOCK
    basis_tile = (
        basis_sum.reshape(3, BLOCK_ROWS, BLOCK_COLS, BLOCK, BLOCK)
        .transpose(0, 1, 3, 2, 4)
        .reshape(3, tile_rows, tile_cols)
    )
    depth_tile = (
        depth_sum.reshape(BLOCK_ROWS, BLOCK_COLS, BLOCK, BLOCK)
        .transpose(0, 2, 1, 3)
        .reshape(tile_rows, tile_cols)
    )
    half_span = TAPS // 2
    column_mix = band_matrix(tile_cols, half_span)
    row_mix = band_matrix(tile_rows, half_span).transpose(0, 2, 1)
    framed = extended(basis_tile, (("exp", 2), ("tile", 1)), half_span)
    across = jnp.einsum("kyp,kpc->kyc", framed, column_mix, precision=lax.Precision.HIGHEST)
    matched = jnp.einsum("kry,kyc->rc", row_mix, across, precision=lax.Precision.HIGHEST)
    denominator = 1.0 + depth_tile
    coadded = matched / denominator
    detection = lax.psum(coadded * coadded * denominator, "band")
    return (coadded[None], detection)


def solution(mesh):
    return jax.shard_map(
        local,
        mesh=mesh,
        in_specs=(
            P(("patch", "band"), "tile", "exp", None, None),
            P(("patch", "band"), "tile", "exp", None, None),
            P(("patch", "band"), "tile", "exp"),
            P(("patch", "band"), "tile", "exp", None),
            P(("patch", "band"), "tile", "exp"),
            P(("patch", "band"), "tile", "exp"),
            P(),
        ),
        out_specs=(P(("patch", "band"), "tile", "exp"), P(("patch", "tile"), "exp")),
        check_vma=False,
    )
```

profile of v0, /device:TPU:0, one launch (start us, length us, event | category | flops | bytes accessed | tf_op | source)
XLA Modules:
  0.0 137.2 jit_solution(16599511198700164798)
XLA Ops:
  7.2 0.7 add_bitcast_fusion
  7.9 0.9 convert_reduce_fusion
  8.8 0.7 multiply_add_fusion.1
  9.5 0.7 select_reduce_fusion.1
  11.0 6.3 %all-to-all-start = ((s32[4,8,2]{1,2,0:T(2,128)}), s32[4,8,2]{1,2,0:T(2,128)S(1)}, u32[]{:S(2)}, u32[]{:S(2)}) async-start(s32[4,8,2]{1,2,0:T(2,128)} %copy.15), calls=%async_computation | async-start | bytes 8192 | tf_op jit(solution)/shard_map/all_to_all | solution.py:92
  17.3 1.5 %subtract_select_fusion = f32[1,1,16,128,128]{4,3,2,1,0:T(8,128)S(1)} fusion(s32[1,1,16,128,128]{4,3,2,1,0:T(8,128)} %param.8), kind=kLoop, calls=%fused_computation.36 | loop fusion | flops 1835008 | bytes 2097152 | tf_op jit(solution)/shard_map/jit(_where)/select_n | solution.py:31
  19.5 2.4 %fusion = bf16[4,8,16384]{2,1,0:T(8,128)(2,1)} fusion(f32[2,8,128,128]{3,2,1,0:T(8,128)S(1)} %convert.1, f32[2,8,128,128]{3,2,1,0:T(8,128)S(1)} %bitcast.88, f32[16]{0:T(128)S(1)} %bitcast.95, s32[16]{0:T(128)S(1)} %multiply_add_fusion.1), kind=kOutput, calls=%fused_computation.2 | convolution fusion | flops 18088448 | bytes 3145856 | tf_op jit(solution)/shard_map/dot_general | solution.py:85
  21.8 1.1 all-to-all-done
  22.9 4.0 %all-to-all-start.1 = ((bf16[4,8,16384]{2,1,0:T(8,128)(2,1)}), bf16[4,8,16384]{2,1,0:T(8,128)(2,1)S(1)}, u32[]{:S(2)}, u32[]{:S(2)}) async-start(bf16[4,8,16384]{2,1,0:T(8,128)(2,1)} %fusion), calls=%async_computation.1 | async-start | bytes 2097152 | tf_op jit(solution)/shard_map/all_to_all | solution.py:90
  26.9 0.6 exponential_reduce_fusion
  28.2 0.6 exponential_reduce_fusion.2
  28.8 1.8 %fusion.1 = bf16[4,8,16384]{2,1,0:T(8,128)(2,1)} fusion(f32[2,8,128,128]{3,2,1,0:T(8,128)S(1)} %bitcast.89, f32[16]{0:T(128)S(1)} %bitcast.96, s32[16]{0:T(128)S(1)} %multiply_add_fusion.1), kind=kOutput, calls=%fused_computation.3 | convolution fusion | flops 17826304 | bytes 2097280 | tf_op jit(solution)/shard_map/dot_general | solution.py:79
  30.6 2.0 %select_divide_fusion.2 = f32[1,552,512]{2,1,0:T(8,128)} fusion(f32[]{:T(128)} %exponential_reduce_fusion.2), kind=kLoop, calls=%fused_computation.26 | loop fusion | flops 2826240 | bytes 1130500 | tf_op jit(solution)/shard_map/div | solution.py:44
  32.6 3.3 %select_divide_fusion = (f32[1,552,512]{2,1,0:T(8,128)}, f32[1,552,512]{2,1,0:T(8,128)}) fusion(f32[]{:T(128)} %exponential_reduce_fusion, f32[]{:T(128)} %exponential_reduce_fusion.1), kind=kLoop, calls=%fused_computation.24 | loop fusion | flops 3674112 | bytes 2261000 | tf_op jit(solution)/shard_map/div | solution.py:44
  35.9 16.2 %all-to-all-done.1 = bf16[4,8,16384]{2,1,0:T(8,128)(2,1)S(1)} async-done(((bf16[4,8,16384]{2,1,0:T(8,128)(2,1)}), bf16[4,8,16384]{2,1,0:T(8,128)(2,1)S(1)}, u32[]{:S(2)}, u32[]{:S(2)}) %all-to-all-start.1) | async-done | bytes 1048608 | tf_op jit(solution)/shard_map/all_to_all | solution.py:90
  52.1 4.3 %all-to-all-start.2 = ((bf16[4,8,16384]{2,1,0:T(8,128)(2,1)}), bf16[4,8,16384]{2,1,0:T(8,128)(2,1)}, u32[]{:S(2)}, u32[]{:S(2)}) async-start(bf16[4,8,16384]{2,1,0:T(8,128)(2,1)} %fusion.1), calls=%async_computation.2 | async-start | bytes 2097152 | tf_op jit(solution)/shard_map/all_to_all | solution.py:91
  56.4 2.2 %select_divide_fusion.3 = (f32[1,296,256]{2,1,0:T(8,128)S(1)}, f32[1,296,256]{2,1,0:T(8,128)}) fusion(f32[]{:T(128)} %exponential_reduce_fusion, f32[]{:T(128)} %exponential_reduce_fusion.1), kind=kLoop, calls=%fused_computation.48 | loop fusion | flops 985088 | bytes 606216 | tf_op jit(solution)/shard_map/div | solution.py:44
  59.2 1.5 %convolution_bitcast_fusion = f32[3,2,128,4,128]{4,3,2,1,0:T(4,128)S(1)} fusion(bf16[128,128,32,1,1]{1,0,2,4,3:T(8,128)(2,1)S(1)} %bitcast.91, f32[2,4,32]{2,1,0:T(4,128)S(1)} %compare_convert_fusion, f32[3,32]{1,0:T(4,128)S(1)} %convolution_bitcast_fusion.2), kind=kOutput, calls=%fused_computation.20 | convolution fusion | flops 150995712 | bytes 2622848 | tf_op jit(solution)/shard_map/kbp,px->kbx/dot_general | solution.py:101
  60.7 0.6 reshape.301
  61.6 1.3 collective-permute-start.1
  62.9 4.6 %collective-permute-start = (f32[3,256,20]{2,1,0:T(8,128)S(1)}, f32[3,256,20]{2,1,0:T(8,128)S(1)}, u32[]{:S(2)}, u32[]{:S(2)}) collective-permute-start(f32[3,256,20]{2,1,0:T(8,128)S(1)} %get-tuple-element.6), channel_id=1, source_target_pairs={{0,4},{4,8},{8,12},{1,5},{5,9},{9,13},{2,6},{6,10},{10,14},{3,7},{... | collective-permute-start | bytes 184328 | tf_op jit(solution)/shard_map/ppermute | solution.py:20
  67.4 0.7 select_divide_fusion.5
  68.2 15.3 %collective-permute-done.1 = f32[3,256,20]{2,1,0:T(8,128)S(1)} collective-permute-done((f32[3,256,20]{2,1,0:T(8,128)S(1)}, f32[3,256,20]{2,1,0:T(8,128)S(1)}, u32[]{:S(2)}, u32[]{:S(2)}) %collective-permute-start.1) | collective-permute-done | bytes 61472 | tf_op jit(solution)/shard_map/ppermute | solution.py:23
  83.5 0.9 pad_maximum_fusion.2
  84.4 1.4 %collective-permute-start.3 = (f32[3,20,552]{2,1,0:T(8,128)}, f32[3,20,552]{2,1,0:T(8,128)}, u32[]{:S(2)}, u32[]{:S(2)}) collective-permute-start(f32[3,20,552]{2,1,0:T(8,128)} %get-tuple-element.5), channel_id=1, source_target_pairs={{2,0},{3,1},{6,4},{7,5},{10,8},{11,9},{14,12},{15,13},{18,16},{19,... | collective-permute-start | bytes 397448 | tf_op jit(solution)/shard_map/ppermute | solution.py:23
  85.8 5.9 %collective-permute-start.2 = (f32[3,20,552]{2,1,0:T(8,128)S(1)}, f32[3,20,552]{2,1,0:T(8,128)}, u32[]{:S(2)}, u32[]{:S(2)}) collective-permute-start(f32[3,20,552]{2,1,0:T(8,128)S(1)} %get-tuple-element.4), channel_id=1, source_target_pairs={{0,2},{1,3},{4,6},{5,7},{8,10},{9,11},{12,14},{13,15},{16,18},{17,... | collective-permute-start | bytes 397448 | tf_op jit(solution)/shard_map/ppermute | solution.py:20
  91.7 1.6 %convolution_add_fusion = f32[2,4,128,128]{3,1,2,0:T(4,128)S(1)} fusion(s32[32]{0:T(128)S(1)} %get-tuple-element.9, s32[2,4]{1,0:T(2,128)S(1)} %multiply_add_fusion, bf16[4,8,16384]{2,1,0:T(8,128)(2,1)} %all-to-all-done.2), kind=kOutput, calls=%fused_computation.22 | convolution fusion | flops 8519936 | bytes 1573024 | tf_op jit(solution)/shard_map/dot_general | solution.py:107
  93.3 0.7 collective-permute-done.2
  94.1 6.7 %fusion.2 = f32[3,296,512]{2,1,0:T(8,128)S(1)} fusion(f32[1,552,512]{2,1,0:T(8,128)} %get-tuple-element.12, f32[1,552,512]{2,1,0:T(8,128)} %get-tuple-element.13, f32[1,552,512]{2,1,0:T(8,128)S(1)} %copy-done.2, f32[3,20,552]{2,1,0:T(8,128)} %collective-permute-done.3, f32[3,256,20]{2,1,0:T(8,128)S(1)} %copy-done.5, f32[3,256,512]{2,1,0:T(8,128)S(1)} %reshape.301, ...), kind=kOutput, calls=%fused_computation.4 | convolution fusion | flops 3015297792 | bytes 7170816 | tf_op jit(solution)/shard_map/kyp,kpc->kyc/dot_general | solution.py:128
  100.7 2.9 %bitcast_multiply_fusion.2 = (f32[256,512]{1,0:T(8,128)}, f32[256,512]{1,0:T(8,128)}) fusion(f32[32,8,4,128]{3,2,1,0:T(4,128)S(1)} %bitcast.92, f32[3,296,512]{2,1,0:T(8,128)S(1)} %fusion.2, f32[1,296,256]{2,1,0:T(8,128)S(1)} %get-tuple-element.14, f32[1,296,256]{2,1,0:T(8,128)S(1)} %copy-done.1, f32[1,296,256]{2,1,0:T(8,128)S(1)} %select_divide_fusion.5), kind=kOutput, calls=%fused_computation.44 | convolution fusion | flops 1397551104 | bytes 4300800 | tf_op jit(solution)/shard_map/kry,kyc->rc/dot_general | solution.py:129
  103.7 24.8 %all-reduce.2.cloned.1.call-done = f32[256,512]{1,0:T(8,128)} async-done(((f32[256,512]{1,0:T(8,128)}), f32[256,512]{1,0:T(8,128)}) %all-reduce.2.cloned.1.call-update) | async-done | bytes 524304 | tf_op jit(solution)/shard_map/psum | solution.py:132
  128.5 1.9 %copy.47 = f32[256,512]{1,0:T(8,128)} copy(f32[256,512]{1,0:T(8,128)} %all-reduce.2.cloned.1.call-done) | data formatting | bytes 1048576
  (36 shorter events, 2.9 us)
Async XLA Ops:
  7.2 51.6 %copy-start = (f32[64,3]{0,1:T(4,128)S(1)}, f32[64,3]{0,1:T(4,128)}, u32[]{:S(2)}) copy-start(f32[64,3]{0,1:T(4,128)} %param.13) | copy-start | bytes 2308
  7.2 11.6 %copy-start.3 = (bf16[1,1,16,128,128]{4,3,2,1,0:T(8,128)(2,1)S(1)}, bf16[1,1,16,128,128]{4,3,2,1,0:T(8,128)(2,1)}, u32[]{:S(2)}) copy-start(bf16[1,1,16,128,128]{4,3,2,1,0:T(8,128)(2,1)} %param.7) | copy-start | bytes 1572868
  11.0 11.9 %all-to-all-start = ((s32[4,8,2]{1,2,0:T(2,128)}), s32[4,8,2]{1,2,0:T(2,128)S(1)}, u32[]{:S(2)}, u32[]{:S(2)}) async-start(s32[4,8,2]{1,2,0:T(2,128)} %copy.15), calls=%async_computation | async-start | bytes 8192 | tf_op jit(solution)/shard_map/all_to_all | solution.py:92
  18.8 0.7 copy-start.7
  22.9 29.2 %all-to-all-start.1 = ((bf16[4,8,16384]{2,1,0:T(8,128)(2,1)}), bf16[4,8,16384]{2,1,0:T(8,128)(2,1)S(1)}, u32[]{:S(2)}, u32[]{:S(2)}) async-start(bf16[4,8,16384]{2,1,0:T(8,128)(2,1)} %fusion), calls=%async_computation.1 | async-start | bytes 2097152 | tf_op jit(solution)/shard_map/all_to_all | solution.py:90
  52.1 39.6 %all-to-all-start.2 = ((bf16[4,8,16384]{2,1,0:T(8,128)(2,1)}), bf16[4,8,16384]{2,1,0:T(8,128)(2,1)}, u32[]{:S(2)}, u32[]{:S(2)}) async-start(bf16[4,8,16384]{2,1,0:T(8,128)(2,1)} %fusion.1), calls=%async_computation.2 | async-start | bytes 2097152 | tf_op jit(solution)/shard_map/all_to_all | solution.py:91
  56.4 72.1 %all-reduce.2.cloned.1.call-start = ((), (), s32[]{:S(2)}) async-start(), calls=%async_computation.3 | async-start | bytes 1048576 | tf_op jit(solution)/shard_map/psum | solution.py:132
  61.6 21.9 %collective-permute-start.1 = (f32[3,256,20]{2,1,0:T(8,128)S(1)}, f32[3,256,20]{2,1,0:T(8,128)S(1)}, u32[]{:S(2)}, u32[]{:S(2)}) collective-permute-start(f32[3,256,20]{2,1,0:T(8,128)S(1)} %get-tuple-element.7), channel_id=1, source_target_pairs={{4,0},{8,4},{12,8},{5,1},{9,5},{13,9},{6,2},{10,6},{14,10},{7,3},{... | collective-permute-start | bytes 184328 | tf_op jit(solution)/shard_map/ppermute | solution.py:23
  62.9 20.6 %collective-permute-start = (f32[3,256,20]{2,1,0:T(8,128)S(1)}, f32[3,256,20]{2,1,0:T(8,128)S(1)}, u32[]{:S(2)}, u32[]{:S(2)}) collective-permute-start(f32[3,256,20]{2,1,0:T(8,128)S(1)} %get-tuple-element.6), channel_id=1, source_target_pairs={{0,4},{4,8},{8,12},{1,5},{5,9},{9,13},{2,6},{6,10},{10,14},{3,7},{... | collective-permute-start | bytes 184328 | tf_op jit(solution)/shard_map/ppermute | solution.py:20
  83.5 0.9 copy-start.4
  83.5 0.9 copy-start.6
  84.4 9.7 %copy-start.2 = (f32[1,552,512]{2,1,0:T(8,128)S(1)}, f32[1,552,512]{2,1,0:T(8,128)}, u32[]{:S(2)}) copy-start(f32[1,552,512]{2,1,0:T(8,128)} %select_divide_fusion.2) | copy-start | bytes 3391492
  84.4 8.9 %collective-permute-start.3 = (f32[3,20,552]{2,1,0:T(8,128)}, f32[3,20,552]{2,1,0:T(8,128)}, u32[]{:S(2)}, u32[]{:S(2)}) collective-permute-start(f32[3,20,552]{2,1,0:T(8,128)} %get-tuple-element.5), channel_id=1, source_target_pairs={{2,0},{3,1},{6,4},{7,5},{10,8},{11,9},{14,12},{15,13},{18,16},{19,... | collective-permute-start | bytes 397448 | tf_op jit(solution)/shard_map/ppermute | solution.py:23
  85.8 8.2 %collective-permute-start.2 = (f32[3,20,552]{2,1,0:T(8,128)S(1)}, f32[3,20,552]{2,1,0:T(8,128)}, u32[]{:S(2)}, u32[]{:S(2)}) collective-permute-start(f32[3,20,552]{2,1,0:T(8,128)S(1)} %get-tuple-element.4), channel_id=1, source_target_pairs={{0,2},{1,3},{4,6},{5,7},{8,10},{9,11},{12,14},{13,15},{16,18},{17,... | collective-permute-start | bytes 397448 | tf_op jit(solution)/shard_map/ppermute | solution.py:20
  91.7 2.4 %copy-start.5 = (f32[3,256,20]{2,1,0:T(8,128)S(1)}, f32[3,256,20]{2,1,0:T(8,128)}, u32[]{:S(2)}) copy-start(f32[3,256,20]{2,1,0:T(8,128)} %copy-done.4) | copy-start | bytes 184324
  94.1 6.7 %copy-start.1 = (f32[1,296,256]{2,1,0:T(8,128)S(1)}, f32[1,296,256]{2,1,0:T(8,128)}, u32[]{:S(2)}) copy-start(f32[1,296,256]{2,1,0:T(8,128)} %get-tuple-element.15) | copy-start | bytes 909316
Sparse Core Ops, SparseCore 0:
  103.8 24.5 all-reduce.1
where the time goes:
time: 138 us; the launch traced here: 137 us
  waiting for transfers between devices  58 us (42%)
  starting transfers between devices  27.8 us (20%)
  matrix products  17 us (12%)
  other arithmetic  15.7 us (11%)
  between operations  14.2 us (10%)
  local copies, waits for them, and re-layouts  4.37 us (3%)
    psum x1, waiting for transfers between devices, local(): detection = lax.psum(coadded * coadded * denominator, 'band')  24.8 us
    all_to_all x1, waiting for transfers between devices, local(): lax.all_to_all(send_weighted, 'exp', split_axis=0, concat_axis=0, tiled=T...  16.2 us
    ppermute x2, waiting for transfers between devices, extended(): lax.ppermute(lax.slice_in_dim(block, 0, width, axis=dim), axis, backward)  15.3 us
    ppermute x2, starting transfers between devices, extended(): lax.ppermute(lax.slice_in_dim(block, block.shape[dim] - width, None, axis...  10.5 us
    div x4, other arithmetic, band_matrix(): jnp.where(inside, jnp.exp(-offset * offset / (2.0 * spread * spread)), 0.0)  8.28 us
    dot_general x1, matrix products, local(): jnp.einsum('kyp,kpc->kyc', framed, column_mix, precision=lax.Precision.HI...  6.67 us
    all_to_all x1, starting transfers between devices, local(): lax.all_to_all(labels, 'exp', split_axis=0, concat_axis=0, tiled=True)  6.32 us
    all_to_all x1, starting transfers between devices, local(): lax.all_to_all(send_weight, 'exp', split_axis=0, concat_axis=0, tiled=True)  4.26 us
  transfers between devices with their start and end apart: 8, of which 5 were waited for; matrix products, arithmetic and copies ran while one was open for 16% of the time, Pallas kernels for 0%

commit v1 on v0

--- a/solution.py
+++ b/solution.py
@@ -1,6 +1,12 @@
+import functools
+
 import jax
 import jax.numpy as jnp
+import ml_dtypes
+import numpy as np
 from jax import lax
+from jax.experimental import pallas as pl
+from jax.experimental.pallas import tpu as pltpu
 from jax.sharding import PartitionSpec as P
 
 BLOCK = 128
@@ -46,7 +52,7 @@
     return jnp.stack(result)
 
 
-def local(images, mask_bits, inv_var, routes, block_slot, kernel_index, coefficients):
+def routed(images, mask_bits, inv_var, routes, block_slot, kernel_index, coefficients):
     peer_count = lax.axis_size("exp")
     held_count = images.shape[2]
     capacity = max(2, 2 * held_count // peer_count)
@@ -131,6 +137,354 @@
     coadded = matched / denominator
     detection = lax.psum(coadded * coadded * denominator, "band")
     return (coadded[None], detection)
+
+
+HALF = TAPS // 2
+EDGE = 32
+REACH = 152
+LINE = 4
+TILE_BLOCKS = BLOCK_ROWS * BLOCK_COLS
+TILE_ROWS = BLOCK_ROWS * BLOCK
+TILE_COLS = BLOCK_COLS * BLOCK
+MEBI = 1024 * 1024
+
+
+def tap_values(offset):
+    span = np.arange(-HALF, HALF + 1, dtype=np.float64)
+    inside = np.abs(offset) <= HALF
+    result = []
+    for spread in kernel_sigmas:
+        total = np.exp(-span * span / (2.0 * spread * spread)).sum()
+        value = np.exp(-offset.astype(np.float64) ** 2 / (2.0 * spread * spread)) / total
+        result.append(np.where(inside, value, 0.0))
+    return np.stack(result)
+
+
+def split_taps(values):
+    high = values.astype(ml_dtypes.bfloat16)
+    low = (values - high.astype(np.float64)).astype(ml_dtypes.bfloat16)
+    return high, low
+
+
+def row_taps(first_row, rows):
+    result = []
+    for block_row in range(BLOCK_ROWS):
+        target = first_row[block_row] + np.arange(rows)[:, None]
+        source = block_row * BLOCK + np.arange(BLOCK)[None, :]
+        values = tap_values(target - source).reshape(3 * rows, BLOCK)
+        result.append(np.concatenate(split_taps(values), axis=1))
+    return np.stack(result)
+
+
+def column_taps():
+    lane = np.arange(BLOCK)
+    beside = np.where(lane < BLOCK // 2, lane + BLOCK, lane - BLOCK)
+    target = np.concatenate([lane, beside])[None, :]
+    high, low = split_taps(tap_values(target - lane[:, None]).reshape(3 * BLOCK, 2 * BLOCK))
+    return np.concatenate([high, high, low], axis=0)
+
+
+def code(value):
+    return (value * jnp.abs(value)).astype(jnp.bfloat16)
+
+
+def decode(coded):
+    square = coded.astype(jnp.float32)
+    root = jnp.sqrt(jnp.abs(square))
+    return jnp.where(square < 0, -root, root)
+
+
+def tile_at(place):
+    me = lax.axis_index("exp")
+    return jnp.where(me < LINE // 2, LINE - 1 - place, place)
+
+
+def split_rows(block, mixing):
+    rows = block.shape[0] // 3
+    high, low = [], []
+    for k in range(3):
+        value = mixing[k] * block[k * rows : (k + 1) * rows]
+        rounded = value.astype(jnp.bfloat16)
+        high.append(rounded)
+        low.append((value - rounded.astype(jnp.float32)).astype(jnp.bfloat16))
+    return jnp.concatenate(high + low + high, axis=1)
+
+
+def spread_columns(target, column, rows, values):
+    beside = values[:, BLOCK:]
+    to_right = lax.broadcasted_iota(jnp.int32, beside.shape, 1) < BLOCK // 2
+    target[column, rows] += values[:, :BLOCK]
+    target[column + 1, rows] += jnp.where(to_right, beside, 0.0)
+    target[column - 1, rows] += jnp.where(to_right, 0.0, beside)
+
+
+def pixel_kernel(held, *refs):
+    (
+        routes_in, slots_in, inverse_in, bits_in, images_in,
+        out_weighted, out_far, out_third, out_last,
+        routes, slots, inverse, bits, images, share, depth, far, sems,
+    ) = refs
+    small = [
+        pltpu.make_async_copy(src, dst, sems.at[n])
+        for n, (src, dst) in enumerate(
+            ((routes_in, routes), (slots_in, slots), (inverse_in, inverse))
+        )
+    ]
+    parts = 4
+    size = held // parts
+    large = [
+        pltpu.make_async_copy(
+            src.at[pl.ds(p * size, size)], dst.at[pl.ds(p * size, size)], sems.at[3 + first + p]
+        )
+        for first, src, dst in ((0, bits_in, bits), (parts, images_in, images))
+        for p in range(parts)
+    ]
+    for copy in small + large:
+        copy.start()
+    depth[...] = jnp.zeros_like(depth)
+    for copy in small:
+        copy.wait()
+    for s in range(held):
+        if s % size == 0:
+            large[s // size].wait()
+        flags = bits[s]
+        full = inverse[s]
+        part = jnp.where((flags & 1) == 1, 0.5 * full, full)
+        part = jnp.where((flags & 6) == 6, 0.0, part)
+        share[s] = part
+        depth[routes[s] * TILE_BLOCKS + slots[s]] += part.astype(jnp.bfloat16).astype(jnp.float32)
+
+    def write_depth(place, ref):
+        tile = tile_at(place)
+        for b in range(TILE_BLOCKS):
+            row, col = b // BLOCK_COLS * BLOCK, b % BLOCK_COLS * BLOCK
+            ref[row : row + BLOCK, col : col + BLOCK] = depth[tile * TILE_BLOCKS + b].astype(
+                jnp.bfloat16
+            )
+
+    for place in range(2):
+        write_depth(place, far.at[place])
+    out_copy = pltpu.make_async_copy(far, out_far, sems.at[3 + 2 * parts])
+    out_copy.start()
+    write_depth(2, out_third)
+    write_depth(3, out_last)
+    for s in range(held):
+        if s % size == 0:
+            large[parts + s // size].wait()
+        out_weighted[s] = (share[s] * images[s].astype(jnp.float32)).astype(jnp.bfloat16)
+    out_copy.wait()
+
+
+def edge_kernel(held, routes, slots, kinds, coefs, weighted, taps, col_taps, out_edge, factors, total):
+    strip = lax.axis_index("tile")
+    total[...] = jnp.zeros_like(total)
+    for s in range(held):
+        pixels = weighted[s]
+        moved = jnp.dot(
+            taps[1 - strip],
+            jnp.concatenate([pixels, pixels], axis=0),
+            preferred_element_type=jnp.float32,
+        )
+        crosses = (slots[s] // BLOCK_COLS == 1 - strip).astype(jnp.float32)
+        factors[s * EDGE : (s + 1) * EDGE] = split_rows(
+            moved, [crosses * coefs[k, kinds[s]] for k in range(3)]
+        )
+    result = jnp.dot(factors[...], col_taps[...], preferred_element_type=jnp.float32)
+    for s in range(held):
+        column = 1 + routes[s] * BLOCK_COLS + slots[s] % BLOCK_COLS
+        spread_columns(total, column, pl.ds(0, EDGE), result[s * EDGE : (s + 1) * EDGE])
+    for place in range(LINE):
+        for b in range(BLOCK_COLS):
+            out_edge[place, :, b * BLOCK : (b + 1) * BLOCK] = total[
+                1 + tile_at(place) * BLOCK_COLS + b
+            ].astype(jnp.bfloat16)
+
+
+def match_kernel(held, *refs):
+    routes, slots, kinds, coefs, weighted, taps, col_taps = refs[:7]
+    out_tiles = refs[7 : 7 + LINE]
+    total = refs[7 + LINE]
+    total[...] = jnp.zeros_like(total)
+    for s in range(held):
+        slot = slots[s]
+        block_row = slot // BLOCK_COLS
+        pixels = weighted[s]
+        moved = jnp.dot(
+            taps[block_row],
+            jnp.concatenate([pixels, pixels], axis=0),
+            preferred_element_type=jnp.float32,
+        )
+        factors = split_rows(moved, [coefs[k, kinds[s]] for k in range(3)])
+        result = jnp.dot(factors, col_taps[...], preferred_element_type=jnp.float32)
+        row = pl.multiple_of(block_row * (TILE_ROWS - REACH), 8)
+        column = 1 + routes[s] * BLOCK_COLS + slot % BLOCK_COLS
+        spread_columns(total, column, pl.ds(row, REACH), result)
+    for place in range(LINE):
+        for b in range(BLOCK_COLS):
+            out_tiles[place][:, b * BLOCK : (b + 1) * BLOCK] = total[
+                1 + tile_at(place) * BLOCK_COLS + b
+            ]
+
+
+def edge_rows():
+    return pl.ds(pl.multiple_of((1 - lax.axis_index("tile")) * (TILE_ROWS - EDGE), EDGE), EDGE)
+
+
+def relay_kernel(own, got, edge, out):
+    rows = edge_rows()
+    out[...] = code(own[...] + decode(got[...]))
+    out[rows] = code(own[rows] + edge[...].astype(jnp.float32) + decode(got[rows]))
+
+
+def final_kernel(
+    third_d, last_d, got_third, got_far_d, got_last_d, third_m, last_m, edge, got_m, got_last_m,
+    out_coadd, out_term, total,
+):
+    me = lax.axis_index("exp")
+    at_end = jnp.logical_or(me == 0, me == LINE - 1)
+    own_m = jnp.where(at_end, last_m[...], third_m[...])
+    total[...] = own_m + decode(got_third[1]) + (decode(got_m[...]) + decode(got_last_m[...]))
+    rows = edge_rows()
+    total[rows] += jnp.where(at_end, edge[3].astype(jnp.float32), edge[2].astype(jnp.float32))
+    own_d = jnp.where(at_end, last_d[...].astype(jnp.float32), third_d[...].astype(jnp.float32))
+    denominator = (
+        (1.0 + own_d)
+        + got_third[0].astype(jnp.float32)
+        + (got_far_d[1].astype(jnp.float32) + got_last_d[...].astype(jnp.float32))
+    )
+    coadd = total[...] / denominator
+    out_coadd[...] = coadd
+    out_term[...] = (coadd * coadd * denominator).astype(jnp.bfloat16)
+
+
+def first_kernel(tile_0, tile_1, tile_2, edge, third_d, far, next_far, third_both):
+    rows = edge_rows()
+    for place, (source, out) in enumerate(((tile_0, far), (tile_1, next_far), (tile_2, third_both.at[1]))):
+        out[...] = code(source[...])
+        out[rows] = code(source[rows] + edge[place].astype(jnp.float32))
+    third_both[0] = third_d[...]
+
+
+def in_vmem(count):
+    return [pl.BlockSpec(memory_space=pltpu.VMEM)] * count
+
+
+def in_smem(count):
+    return [pl.BlockSpec(memory_space=pltpu.SMEM)] * count
+
+
+def in_hbm(count):
+    return [pl.BlockSpec(memory_space=pltpu.HBM)] * count
+
+
+def vmem_limit(mebibytes):
+    return pltpu.CompilerParams(vmem_limit_bytes=mebibytes * MEBI)
+
+
+def reduced(images, mask_bits, inv_var, routes, block_slot, kernel_index, coefficients):
+    held = images.shape[2]
+    tile = jax.ShapeDtypeStruct((TILE_ROWS, TILE_COLS), jnp.bfloat16)
+    wide = jax.ShapeDtypeStruct((TILE_ROWS, TILE_COLS), jnp.float32)
+    pair = jax.ShapeDtypeStruct((2, TILE_ROWS, TILE_COLS), jnp.bfloat16)
+    columns = LINE * BLOCK_COLS + 2
+    target, slot, kind = routes.reshape(held), block_slot.reshape(held), kernel_index.reshape(held)
+    mixing = coefficients.T
+    inward = [(0, 1), (LINE - 1, LINE - 2)]
+    across = [(1, 2), (2, 1)]
+    outward = [(1, 0), (LINE - 2, LINE - 1)]
+
+    weighted, far_d, third_d, last_d = pl.pallas_call(
+        functools.partial(pixel_kernel, held),
+        out_shape=[jax.ShapeDtypeStruct((held, BLOCK, BLOCK), jnp.bfloat16), pair, tile, tile],
+        in_specs=in_hbm(5),
+        out_specs=in_vmem(1) + in_hbm(1) + in_vmem(2),
+        scratch_shapes=[
+            pltpu.SMEM((held,), jnp.int32),
+            pltpu.SMEM((held,), jnp.int32),
+            pltpu.SMEM((held,), jnp.float32),
+            pltpu.VMEM((held, BLOCK, BLOCK), jnp.int32),
+            pltpu.VMEM((held, BLOCK, BLOCK), jnp.bfloat16),
+            pltpu.VMEM((held, BLOCK, BLOCK), jnp.float32),
+            pltpu.VMEM((LINE * TILE_BLOCKS, BLOCK, BLOCK), jnp.float32),
+            pltpu.VMEM((2, TILE_ROWS, TILE_COLS), jnp.bfloat16),
+            pltpu.SemaphoreType.DMA((12,)),
+        ],
+        compiler_params=vmem_limit(24),
+        name="pixels",
+    )(target, slot, inv_var.reshape(held), mask_bits[0, 0], images[0, 0])
+    got_far_d = lax.ppermute(far_d, "exp", inward)
+
+    col_taps = jnp.asarray(column_taps())
+    edge = pl.pallas_call(
+        functools.partial(edge_kernel, held),
+        out_shape=jax.ShapeDtypeStruct((LINE, EDGE, TILE_COLS), jnp.bfloat16),
+        in_specs=in_smem(4) + in_vmem(3),
+        out_specs=pl.BlockSpec(memory_space=pltpu.VMEM),
+        scratch_shapes=[
+            pltpu.VMEM((held * EDGE, 9 * BLOCK), jnp.bfloat16),
+            pltpu.VMEM((columns, EDGE, BLOCK), jnp.float32),
+        ],
+        compiler_params=vmem_limit(24),
+        name="edges",
+    )(target, slot, kind, mixing, weighted, jnp.asarray(row_taps((-EDGE, TILE_ROWS), EDGE)), col_taps)
+    other_edge = lax.ppermute(edge, "tile", [(0, 1), (1, 0)])
+
+    own_m = pl.pallas_call(
+        functools.partial(match_kernel, held),
+        out_shape=[wide] * LINE,
+        in_specs=in_smem(4) + in_vmem(3),
+        out_specs=in_vmem(LINE),
+        scratch_shapes=[pltpu.VMEM((columns, TILE_ROWS, BLOCK), jnp.float32)],
+        compiler_params=vmem_limit(24),
+        name="match",
+    )(target, slot, kind, mixing, weighted, jnp.asarray(row_taps((0, TILE_ROWS - REACH), REACH)), col_taps)
+    far_m, next_m, third_both = pl.pallas_call(
+        first_kernel,
+        out_shape=[tile, tile, pair],
+        in_specs=in_vmem(5),
+        out_specs=in_vmem(3),
+        compiler_params=vmem_limit(24),
+        name="first",
+    )(*own_m[:3], other_edge, third_d)
+
+    def relay(own, got, place):
+        return pl.pallas_call(
+            relay_kernel,
+            out_shape=tile,
+            in_specs=in_vmem(3),
+            out_specs=pl.BlockSpec(memory_space=pltpu.VMEM),
+            compiler_params=vmem_limit(24),
+            name="relay",
+        )(own, got, other_edge[place])
+
+    got_far_m = lax.ppermute(far_m, "exp", inward)
+    mid_d = lax.ppermute(far_d + got_far_d, "exp", across)
+    got_next_m = lax.ppermute(next_m, "exp", inward)
+    mid_far_m = lax.ppermute(relay(own_m[0], got_far_m, 0), "exp", across)
+    got_third = lax.ppermute(third_both, "exp", inward)
+    end_d = lax.ppermute(last_d + mid_d[0], "exp", outward)
+    mid_m = lax.ppermute(relay(own_m[1], got_next_m, 1), "exp", across)
+    end_m = lax.ppermute(relay(own_m[3], mid_far_m, 3), "exp", outward)
+    coadd, term = pl.pallas_call(
+        final_kernel,
+        out_shape=[wide, tile],
+        in_specs=in_vmem(10),
+        out_specs=in_vmem(2),
+        scratch_shapes=[pltpu.VMEM((TILE_ROWS, TILE_COLS), jnp.float32)],
+        compiler_params=vmem_limit(24),
+        name="final",
+    )(third_d, last_d, got_third, mid_d, end_d, own_m[2], own_m[3], other_edge, mid_m, end_m)
+    other_term = lax.ppermute(term, "band", [(0, 1), (1, 0)])
+    detection = term.astype(jnp.float32) + other_term.astype(jnp.float32)
+    return (coadd[None], detection)
+
+
+def local(images, mask_bits, inv_var, routes, block_slot, kernel_index, coefficients):
+    peers = lax.axis_size("exp")
+    partial_sums_fit = peers * TILE_BLOCKS <= 2 * images.shape[2]
+    pairs = lax.axis_size("tile") == 2 and lax.axis_size("band") == 2
+    plan = reduced if partial_sums_fit and pairs and peers == LINE else routed
+    return plan(images, mask_bits, inv_var, routes, block_slot, kernel_index, coefficients)
 
 
 def solution(mesh):

time: 138 us -> 60.7 us (0.44)
  waiting for transfers between devices: 58 us -> 20.8 us
  matrix products: 17 us -> 0 us
  other arithmetic: 15.7 us -> 1.03 us
  between operations: 14.2 us -> 0.88 us
  Pallas kernels: 0 us -> 10.8 us
  starting transfers between devices: 27.8 us -> 23.3 us
    psum x1 -> x0, waiting for transfers between devices: 24.8 us -> none  [local(): detection = lax.psum(coadded * coadded * denominator, 'band')]
    all_to_all x3 -> x0, waiting for transfers between devices: 17.2 us -> none  [the longest x1 16.2 us: local(): lax.all_to_all(send_weighted, 'exp', split_axis=0, concat_axis=0, tiled=T...]
    dot_general x7 -> x0, matrix products: 17 us -> none  [the longest x1 6.67 us: local(): jnp.einsum('kyp,kpc->kyc', framed, column_mix, precision=lax.Precision.HI...]
    all_to_all x3 -> x0, starting transfers between devices: 14.6 us -> none  [the longest x1 6.32 us: local(): lax.all_to_all(labels, 'exp', split_axis=0, concat_axis=0, tiled=True)]
    pallas_call x0 -> x8, Pallas kernels: none -> 10.8 us  [the longest x1 4.54 us: reduced(): pl.pallas_call(functools.partial(match_kernel, held), out_shape=[wide] *...]
    ppermute x4 -> x11, starting transfers between devices: 13.2 us -> 23.3 us  [the longest x1 7.19 us: reduced(): got_next_m = lax.ppermute(next_m, 'exp', inward)]
    div x4 -> x0, other arithmetic: 8.28 us -> none  [band_matrix(): jnp.where(inside, jnp.exp(-offset * offset / (2.0 * spread * spread)), 0.0)]
    ppermute x4 -> x11, waiting for transfers between devices: 16.1 us -> 20.8 us  [the longest x1 7.39 us: reduced(): end_m = lax.ppermute(relay(own_m[3], mid_far_m, 3), 'exp', outward)]
  transfers between devices with their start and end apart: 8 -> 11, of which waited for: 5 -> 5; matrix products, arithmetic and copies ran while one was open for 16% -> 0% of each run, Pallas kernels for 0% -> 12%
where the time goes in v1:
time: 60.7 us; the launch traced here: 60.4 us
  starting transfers between devices  23.3 us (38%)
  waiting for transfers between devices  20.8 us (34%)
  Pallas kernels  10.8 us (18%)
  local copies, waits for them, and re-layouts  3.6 us (6%)
  other arithmetic  1.03 us (2%)
  between operations  0.88 us (1%)
    ppermute x1, waiting for transfers between devices, reduced(): end_m = lax.ppermute(relay(own_m[3], mid_far_m, 3), 'exp', outward)  7.39 us
    ppermute x1, starting transfers between devices, reduced(): got_next_m = lax.ppermute(next_m, 'exp', inward)  7.19 us
    ppermute x1, waiting for transfers between devices, reduced(): got_third = lax.ppermute(third_both, 'exp', inward)  6.44 us
    ppermute x1, starting transfers between devices, reduced(): got_far_d = lax.ppermute(far_d, 'exp', inward)  4.96 us
    pallas_call x1, Pallas kernels, reduced(): pl.pallas_call(functools.partial(match_kernel, held), out_shape=[wide] *...  4.54 us
    ppermute x1, starting transfers between devices, reduced(): got_third = lax.ppermute(third_both, 'exp', inward)  3.62 us
    unnamed x20, local copies, waits for them, and re-layouts  3.59 us
    ppermute x1, waiting for transfers between devices, reduced(): end_d = lax.ppermute(last_d + mid_d[0], 'exp', outward)  2.81 us
  transfers between devices with their start and end apart: 11, of which 5 were waited for; matrix products, arithmetic and copies ran while one was open for 0% of the time, Pallas kernels for 12%

profile of v1, /device:TPU:0, one launch (start us, length us, event | category | flops | bytes accessed | tf_op | source)
XLA Modules:
  0.0 60.4 jit_solution(7543068123575751495)
XLA Ops:
  0.7 0.6 %copy-done.6 = s32[1,1,16,1]{2,3,1,0:T(1,128)S(1)} copy-done((s32[1,1,16,1]{2,3,1,0:T(1,128)S(1)}, s32[1,1,16,1]{2,3,1,0:T(1,128)}, u32[]{:S(2)}) %copy-start.6) | copy-done | bytes 88
  1.3 0.0 copy-done.7
  1.3 0.0 copy-done.9
  1.3 1.2 %copy-done.1 = s32[1,1,16,128,128]{4,3,2,1,0:T(8,128)S(1)} copy-done((s32[1,1,16,128,128]{4,3,2,1,0:T(8,128)S(1)}, s32[1,1,16,128,128]{4,3,2,1,0:T(8,128)}, u32[]{:S(2)}) %copy-start.1) | copy-done | bytes 1048600
  2.5 1.0 %copy-done.2 = bf16[1,1,16,128,128]{4,3,2,1,0:T(8,128)(2,1)S(1)} copy-done((bf16[1,1,16,128,128]{4,3,2,1,0:T(8,128)(2,1)S(1)}, bf16[1,1,16,128,128]{4,3,2,1,0:T(8,128)(2,1)}, u32[]{:S(2)}) %copy-start.2) | copy-done | bytes 524312
  3.6 1.6 %pixels.1 = (bf16[16,128,128]{2,1,0:T(8,128)(2,1)S(1)}, bf16[2,256,512]{2,1,0:T(8,128)(2,1)S(1)}, bf16[256,512]{1,0:T(8,128)(2,1)S(1)}, bf16[256,512]{1,0:T(8,128)(2,1)S(1)}) custom-call(s32[16]{0:T(128)S(1)} %bitcast.22, s32[16]{0:T(128)S(1)} %bitcast.25, f32[16]{0:T(128)S(1)} %bitcast.30, s32[16,128,128]{2,1,0:T(8,128)S(1)} %bitcast.18, ...), custom_call_target="tpu_custom_call" | custom-call | tf_op jit(solution)/shard_map/pixels/pallas_call | solution.py:396
  5.2 5.0 %collective-permute-start.2 = (bf16[2,256,512]{2,1,0:T(8,128)(2,1)S(1)}, bf16[2,256,512]{2,1,0:T(8,128)(2,1)S(1)}, u32[]{:S(2)}, u32[]{:S(2)}) collective-permute-start(bf16[2,256,512]{2,1,0:T(8,128)(2,1)S(1)} %get-tuple-element.22), channel_id=1, source_target_pairs={{0,4},{12,8},{1,5},{13,9},{2,6},{14,10},{3,7},{15,11},{16,20},{28,... | collective-permute-start | bytes 1572872 | tf_op jit(solution)/shard_map/ppermute | solution.py:415
  10.2 0.0 copy-start.5
  10.2 0.6 %copy-done.5 = f32[64,3]{0,1:T(4,128)S(1)} copy-done((f32[64,3]{0,1:T(4,128)S(1)}, f32[64,3]{0,1:T(4,128)}, u32[]{:S(2)}) %copy-start.5) | copy-done | bytes 792
  10.9 1.4 %edges.1 = bf16[4,32,512]{2,1,0:T(8,128)(2,1)S(1)} custom-call(s32[16]{0:T(128)S(1)} %bitcast.23, s32[16]{0:T(128)S(1)} %bitcast.26, s32[16]{0:T(128)S(1)} %bitcast.28, f32[3,64]{1,0:T(4,128)S(1)} %bitcast.20, bf16[16,128,128]{2,1,0:T(8,128)(2,1)S(1)} %get-tuple-element.17.refs_4_.weighted, bf16[2,96,256]{2,1,0:T(8,128)(2,1)S(1)} %copy-done.4, ...), custom_call_target="tpu_custom_call" | custom-call | tf_op jit(solution)/shard_map/edges/pallas_call | solution.py:418
  12.3 1.6 %collective-permute-start = (bf16[4,32,512]{2,1,0:T(8,128)(2,1)S(1)}, bf16[4,32,512]{2,1,0:T(8,128)(2,1)S(1)}, u32[]{:S(2)}, u32[]{:S(2)}) collective-permute-start(bf16[4,32,512]{2,1,0:T(8,128)(2,1)S(1)} %edges.1), channel_id=1, source_target_pairs={{0,2},{2,0},{1,3},{3,1},{4,6},{6,4},{5,7},{7,5},{8,10},{10,8},{9,1... | collective-permute-start | bytes 393224 | tf_op jit(solution)/shard_map/ppermute | solution.py:430
  13.8 4.5 %match.1 = (f32[256,512]{1,0:T(8,128)S(1)}, f32[256,512]{1,0:T(8,128)S(1)}, f32[256,512]{1,0:T(8,128)S(1)}, f32[256,512]{1,0:T(8,128)S(1)}) custom-call(s32[16]{0:T(128)S(1)} %bitcast.24, s32[16]{0:T(128)S(1)} %bitcast.27, s32[16]{0:T(128)S(1)} %bitcast.29, f32[3,64]{1,0:T(4,128)S(1)} %bitcast.21, ...), custom_call_target="tpu_custom_call" | custom-call | tf_op jit(solution)/shard_map/match/pallas_call | solution.py:432
  18.4 0.2 first.1
  18.6 1.3 %collective-permute-start.7 = (bf16[256,512]{1,0:T(8,128)(2,1)S(1)}, bf16[256,512]{1,0:T(8,128)(2,1)S(1)}, u32[]{:S(2)}, u32[]{:S(2)}) collective-permute-start(bf16[256,512]{1,0:T(8,128)(2,1)S(1)} %get-tuple-element.25), channel_id=1, source_target_pairs={{0,4},{12,8},{1,5},{13,9},{2,6},{14,10},{3,7},{15,11},{16,20},{28,... | collective-permute-start | bytes 786440 | tf_op jit(solution)/shard_map/ppermute | solution.py:460
  19.9 2.6 %collective-permute-done.2 = bf16[2,256,512]{2,1,0:T(8,128)(2,1)S(1)} collective-permute-done((bf16[2,256,512]{2,1,0:T(8,128)(2,1)S(1)}, bf16[2,256,512]{2,1,0:T(8,128)(2,1)S(1)}, u32[]{:S(2)}, u32[]{:S(2)}) %collective-permute-start.2) | collective-permute-done | bytes 524320 | tf_op jit(solution)/shard_map/ppermute | solution.py:415
  22.5 0.1 add.9
  22.6 0.7 %collective-permute-start.3 = (bf16[2,256,512]{2,1,0:T(8,128)(2,1)S(1)}, bf16[2,256,512]{2,1,0:T(8,128)(2,1)S(1)}, u32[]{:S(2)}, u32[]{:S(2)}) collective-permute-start(bf16[2,256,512]{2,1,0:T(8,128)(2,1)S(1)} %add.9), channel_id=1, source_target_pairs={{4,8},{8,4},{5,9},{9,5},{6,10},{10,6},{7,11},{11,7},{20,24},{24,20... | collective-permute-start | bytes 1572872 | tf_op jit(solution)/shard_map/ppermute | solution.py:461
  23.3 7.2 %collective-permute-start.5 = (bf16[256,512]{1,0:T(8,128)(2,1)S(1)}, bf16[256,512]{1,0:T(8,128)(2,1)S(1)}, u32[]{:S(2)}, u32[]{:S(2)}) collective-permute-start(bf16[256,512]{1,0:T(8,128)(2,1)S(1)} %get-tuple-element.24), channel_id=1, source_target_pairs={{0,4},{12,8},{1,5},{13,9},{2,6},{14,10},{3,7},{15,11},{16,20},{28,... | collective-permute-start | bytes 786440 | tf_op jit(solution)/shard_map/ppermute | solution.py:462
  30.5 0.3 relay.4
  30.8 0.7 %collective-permute-start.8 = (bf16[256,512]{1,0:T(8,128)(2,1)S(1)}, bf16[256,512]{1,0:T(8,128)(2,1)S(1)}, u32[]{:S(2)}, u32[]{:S(2)}) collective-permute-start(bf16[256,512]{1,0:T(8,128)(2,1)S(1)} %relay.4), channel_id=1, source_target_pairs={{4,8},{8,4},{5,9},{9,5},{6,10},{10,6},{7,11},{11,7},{20,24},{24,20... | collective-permute-start | bytes 786440 | tf_op jit(solution)/shard_map/ppermute | solution.py:463
  31.5 3.6 %collective-permute-start.1 = (bf16[2,256,512]{2,1,0:T(8,128)(2,1)S(1)}, bf16[2,256,512]{2,1,0:T(8,128)(2,1)S(1)}, u32[]{:S(2)}, u32[]{:S(2)}) collective-permute-start(bf16[2,256,512]{2,1,0:T(8,128)(2,1)S(1)} %get-tuple-element.21), channel_id=1, source_target_pairs={{0,4},{12,8},{1,5},{13,9},{2,6},{14,10},{3,7},{15,11},{16,20},{28,... | collective-permute-start | bytes 1572872 | tf_op jit(solution)/shard_map/ppermute | solution.py:464
  35.2 0.3 relay.3
  35.5 0.7 %collective-permute-start.6 = (bf16[256,512]{1,0:T(8,128)(2,1)S(1)}, bf16[256,512]{1,0:T(8,128)(2,1)S(1)}, u32[]{:S(2)}, u32[]{:S(2)}) collective-permute-start(bf16[256,512]{1,0:T(8,128)(2,1)S(1)} %relay.3), channel_id=1, source_target_pairs={{4,8},{8,4},{5,9},{9,5},{6,10},{10,6},{7,11},{11,7},{20,24},{24,20... | collective-permute-start | bytes 786440 | tf_op jit(solution)/shard_map/ppermute | solution.py:466
  36.2 0.3 relay.5
  36.5 1.3 %collective-permute-start.9 = (bf16[256,512]{1,0:T(8,128)(2,1)S(1)}, bf16[256,512]{1,0:T(8,128)(2,1)S(1)}, u32[]{:S(2)}, u32[]{:S(2)}) collective-permute-start(bf16[256,512]{1,0:T(8,128)(2,1)S(1)} %relay.5), channel_id=1, source_target_pairs={{4,0},{8,12},{5,1},{9,13},{6,2},{10,14},{7,3},{11,15},{20,16},{24,... | collective-permute-start | bytes 786440 | tf_op jit(solution)/shard_map/ppermute | solution.py:467
  37.8 1.3 %collective-permute-start.4 = (bf16[256,512]{1,0:T(8,128)(2,1)S(1)}, bf16[256,512]{1,0:T(8,128)(2,1)S(1)}, u32[]{:S(2)}, u32[]{:S(2)}) collective-permute-start(bf16[256,512]{1,0:T(8,128)(2,1)S(1)} %fusion), channel_id=1, source_target_pairs={{4,0},{8,12},{5,1},{9,13},{6,2},{10,14},{7,3},{11,15},{20,16},{24,... | collective-permute-start | bytes 786440 | tf_op jit(solution)/shard_map/ppermute | solution.py:465
  39.1 6.4 %collective-permute-done.1.got_third = bf16[2,256,512]{2,1,0:T(8,128)(2,1)S(1)} collective-permute-done((bf16[2,256,512]{2,1,0:T(8,128)(2,1)S(1)}, bf16[2,256,512]{2,1,0:T(8,128)(2,1)S(1)}, u32[]{:S(2)}, u32[]{:S(2)}) %collective-permute-start.1) | collective-permute-done | bytes 524320 | tf_op jit(solution)/shard_map/ppermute | solution.py:464
  45.6 7.4 %collective-permute-done.9.got_last_m = bf16[256,512]{1,0:T(8,128)(2,1)S(1)} collective-permute-done((bf16[256,512]{1,0:T(8,128)(2,1)S(1)}, bf16[256,512]{1,0:T(8,128)(2,1)S(1)}, u32[]{:S(2)}, u32[]{:S(2)}) %collective-permute-start.9) | collective-permute-done | bytes 262176 | tf_op jit(solution)/shard_map/ppermute | solution.py:467
  53.0 2.8 %collective-permute-done.4.got_last_d = bf16[256,512]{1,0:T(8,128)(2,1)S(1)} collective-permute-done((bf16[256,512]{1,0:T(8,128)(2,1)S(1)}, bf16[256,512]{1,0:T(8,128)(2,1)S(1)}, u32[]{:S(2)}, u32[]{:S(2)}) %collective-permute-start.4) | collective-permute-done | bytes 262176 | tf_op jit(solution)/shard_map/ppermute | solution.py:465
  55.8 2.2 %final.1 = (f32[256,512]{1,0:T(8,128)}, bf16[256,512]{1,0:T(8,128)(2,1)S(1)}) custom-call(bf16[256,512]{1,0:T(8,128)(2,1)S(1)} %get-tuple-element.15.third_d, bf16[256,512]{1,0:T(8,128)(2,1)S(1)} %get-tuple-element.16.last_d, bf16[2,256,512]{2,1,0:T(8,128)(2,1)S(1)} %collective-permute-done.1.got_third, ...), custom_call_target="tpu_custom_call" | custom-call | tf_op jit(solution)/shard_map/final/pallas_call | solution.py:468
  58.0 1.5 %collective-permute-done.10 = bf16[256,512]{1,0:T(8,128)(2,1)S(1)} collective-permute-done((bf16[256,512]{1,0:T(8,128)(2,1)S(1)}, bf16[256,512]{1,0:T(8,128)(2,1)S(1)}, u32[]{:S(2)}, u32[]{:S(2)}) %collective-permute-start.10) | collective-permute-done | bytes 262176 | tf_op jit(solution)/shard_map/ppermute | solution.py:477
  59.5 0.9 %convert_add_fusion = f32[256,512]{1,0:T(8,128)} fusion(bf16[256,512]{1,0:T(8,128)(2,1)S(1)} %collective-permute-done.10, bf16[256,512]{1,0:T(8,128)(2,1)S(1)} %get-tuple-element.27), kind=kLoop, calls=%fused_computation | loop fusion | flops 393216 | bytes 1048576 | tf_op jit(solution)/shard_map/add | solution.py:478
  (22 shorter events, 0.1 us)
Async XLA Ops:
  0.6 0.7 %copy-start.6 = (s32[1,1,16,1]{2,3,1,0:T(1,128)S(1)}, s32[1,1,16,1]{2,3,1,0:T(1,128)}, u32[]{:S(2)}) copy-start(s32[1,1,16,1]{2,3,1,0:T(1,128)} %param.13) | copy-start | bytes 196
  0.6 0.7 %copy-start.7 = (s32[1,1,16]{2,1,0:T(1,128)S(1)}, s32[1,1,16]{2,1,0:T(1,128)}, u32[]{:S(2)}) copy-start(s32[1,1,16]{2,1,0:T(1,128)} %param.14) | copy-start | bytes 196
  0.7 0.7 %copy-start.9 = (f32[1,1,16]{2,1,0:T(1,128)S(1)}, f32[1,1,16]{2,1,0:T(1,128)}, u32[]{:S(2)}) copy-start(f32[1,1,16]{2,1,0:T(1,128)} %param.12) | copy-start | bytes 196
  1.3 1.2 %copy-start.1 = (s32[1,1,16,128,128]{4,3,2,1,0:T(8,128)S(1)}, s32[1,1,16,128,128]{4,3,2,1,0:T(8,128)}, u32[]{:S(2)}) copy-start(s32[1,1,16,128,128]{4,3,2,1,0:T(8,128)} %param.11) | copy-start | bytes 3145732
  2.5 1.0 %copy-start.2 = (bf16[1,1,16,128,128]{4,3,2,1,0:T(8,128)(2,1)S(1)}, bf16[1,1,16,128,128]{4,3,2,1,0:T(8,128)(2,1)}, u32[]{:S(2)}) copy-start(bf16[1,1,16,128,128]{4,3,2,1,0:T(8,128)(2,1)} %param.10) | copy-start | bytes 1572868
  3.6 6.6 %copy-start = (bf16[1152,256]{1,0:T(8,128)(2,1)S(1)}, bf16[1152,256]{1,0:T(8,128)(2,1)}, u32[]{:S(2)}) copy-start(bf16[1152,256]{1,0:T(8,128)(2,1)} %constant.6.clone.refs_6_.col_taps) | copy-start | bytes 1769476
  3.6 6.6 %copy-start.4 = (bf16[2,96,256]{2,1,0:T(8,128)(2,1)S(1)}, bf16[2,96,256]{2,1,0:T(8,128)(2,1)}, u32[]{:S(2)}) copy-start(bf16[2,96,256]{2,1,0:T(8,128)(2,1)} %constant.7.clone.taps) | copy-start | bytes 294916
  5.2 17.2 %collective-permute-start.2 = (bf16[2,256,512]{2,1,0:T(8,128)(2,1)S(1)}, bf16[2,256,512]{2,1,0:T(8,128)(2,1)S(1)}, u32[]{:S(2)}, u32[]{:S(2)}) collective-permute-start(bf16[2,256,512]{2,1,0:T(8,128)(2,1)S(1)} %get-tuple-element.22), channel_id=1, source_target_pairs={{0,4},{12,8},{1,5},{13,9},{2,6},{14,10},{3,7},{15,11},{16,20},{28,... | collective-permute-start | bytes 1572872 | tf_op jit(solution)/shard_map/ppermute | solution.py:415
  10.2 0.7 %copy-start.5 = (f32[64,3]{0,1:T(4,128)S(1)}, f32[64,3]{0,1:T(4,128)}, u32[]{:S(2)}) copy-start(f32[64,3]{0,1:T(4,128)} %param.16) | copy-start | bytes 2308
  10.2 0.7 %copy-start.8 = (s32[1,1,16]{2,1,0:T(1,128)S(1)}, s32[1,1,16]{2,1,0:T(1,128)}, u32[]{:S(2)}) copy-start(s32[1,1,16]{2,1,0:T(1,128)} %param.15) | copy-start | bytes 196
  10.9 3.0 %copy-start.3 = (bf16[2,456,256]{2,1,0:T(8,128)(2,1)S(1)}, bf16[2,456,256]{2,1,0:T(8,128)(2,1)}, u32[]{:S(2)}) copy-start(bf16[2,456,256]{2,1,0:T(8,128)(2,1)} %constant.8.clone.refs_5_) | copy-start | bytes 1400836
  12.3 6.1 %collective-permute-start = (bf16[4,32,512]{2,1,0:T(8,128)(2,1)S(1)}, bf16[4,32,512]{2,1,0:T(8,128)(2,1)S(1)}, u32[]{:S(2)}, u32[]{:S(2)}) collective-permute-start(bf16[4,32,512]{2,1,0:T(8,128)(2,1)S(1)} %edges.1), channel_id=1, source_target_pairs={{0,2},{2,0},{1,3},{3,1},{4,6},{6,4},{5,7},{7,5},{8,10},{10,8},{9,1... | collective-permute-start | bytes 393224 | tf_op jit(solution)/shard_map/ppermute | solution.py:430
  18.6 12.0 %collective-permute-start.7 = (bf16[256,512]{1,0:T(8,128)(2,1)S(1)}, bf16[256,512]{1,0:T(8,128)(2,1)S(1)}, u32[]{:S(2)}, u32[]{:S(2)}) collective-permute-start(bf16[256,512]{1,0:T(8,128)(2,1)S(1)} %get-tuple-element.25), channel_id=1, source_target_pairs={{0,4},{12,8},{1,5},{13,9},{2,6},{14,10},{3,7},{15,11},{16,20},{28,... | collective-permute-start | bytes 786440 | tf_op jit(solution)/shard_map/ppermute | solution.py:460
  22.6 15.2 %collective-permute-start.3 = (bf16[2,256,512]{2,1,0:T(8,128)(2,1)S(1)}, bf16[2,256,512]{2,1,0:T(8,128)(2,1)S(1)}, u32[]{:S(2)}, u32[]{:S(2)}) collective-permute-start(bf16[2,256,512]{2,1,0:T(8,128)(2,1)S(1)} %add.9), channel_id=1, source_target_pairs={{4,8},{8,4},{5,9},{9,5},{6,10},{10,6},{7,11},{11,7},{20,24},{24,20... | collective-permute-start | bytes 1572872 | tf_op jit(solution)/shard_map/ppermute | solution.py:461
  23.3 11.9 %collective-permute-start.5 = (bf16[256,512]{1,0:T(8,128)(2,1)S(1)}, bf16[256,512]{1,0:T(8,128)(2,1)S(1)}, u32[]{:S(2)}, u32[]{:S(2)}) collective-permute-start(bf16[256,512]{1,0:T(8,128)(2,1)S(1)} %get-tuple-element.24), channel_id=1, source_target_pairs={{0,4},{12,8},{1,5},{13,9},{2,6},{14,10},{3,7},{15,11},{16,20},{28,... | collective-permute-start | bytes 786440 | tf_op jit(solution)/shard_map/ppermute | solution.py:462
  30.8 5.3 %collective-permute-start.8 = (bf16[256,512]{1,0:T(8,128)(2,1)S(1)}, bf16[256,512]{1,0:T(8,128)(2,1)S(1)}, u32[]{:S(2)}, u32[]{:S(2)}) collective-permute-start(bf16[256,512]{1,0:T(8,128)(2,1)S(1)} %relay.4), channel_id=1, source_target_pairs={{4,8},{8,4},{5,9},{9,5},{6,10},{10,6},{7,11},{11,7},{20,24},{24,20... | collective-permute-start | bytes 786440 | tf_op jit(solution)/shard_map/ppermute | solution.py:463
  31.5 14.1 %collective-permute-start.1 = (bf16[2,256,512]{2,1,0:T(8,128)(2,1)S(1)}, bf16[2,256,512]{2,1,0:T(8,128)(2,1)S(1)}, u32[]{:S(2)}, u32[]{:S(2)}) collective-permute-start(bf16[2,256,512]{2,1,0:T(8,128)(2,1)S(1)} %get-tuple-element.21), channel_id=1, source_target_pairs={{0,4},{12,8},{1,5},{13,9},{2,6},{14,10},{3,7},{15,11},{16,20},{28,... | collective-permute-start | bytes 1572872 | tf_op jit(solution)/shard_map/ppermute | solution.py:464
  35.5 3.7 %collective-permute-start.6 = (bf16[256,512]{1,0:T(8,128)(2,1)S(1)}, bf16[256,512]{1,0:T(8,128)(2,1)S(1)}, u32[]{:S(2)}, u32[]{:S(2)}) collective-permute-start(bf16[256,512]{1,0:T(8,128)(2,1)S(1)} %relay.3), channel_id=1, source_target_pairs={{4,8},{8,4},{5,9},{9,5},{6,10},{10,6},{7,11},{11,7},{20,24},{24,20... | collective-permute-start | bytes 786440 | tf_op jit(solution)/shard_map/ppermute | solution.py:466
  36.5 16.5 %collective-permute-start.9 = (bf16[256,512]{1,0:T(8,128)(2,1)S(1)}, bf16[256,512]{1,0:T(8,128)(2,1)S(1)}, u32[]{:S(2)}, u32[]{:S(2)}) collective-permute-start(bf16[256,512]{1,0:T(8,128)(2,1)S(1)} %relay.5), channel_id=1, source_target_pairs={{4,0},{8,12},{5,1},{9,13},{6,2},{10,14},{7,3},{11,15},{20,16},{24,... | collective-permute-start | bytes 786440 | tf_op jit(solution)/shard_map/ppermute | solution.py:467
  37.8 18.0 %collective-permute-start.4 = (bf16[256,512]{1,0:T(8,128)(2,1)S(1)}, bf16[256,512]{1,0:T(8,128)(2,1)S(1)}, u32[]{:S(2)}, u32[]{:S(2)}) collective-permute-start(bf16[256,512]{1,0:T(8,128)(2,1)S(1)} %fusion), channel_id=1, source_target_pairs={{4,0},{8,12},{5,1},{9,13},{6,2},{10,14},{7,3},{11,15},{20,16},{24,... | collective-permute-start | bytes 786440 | tf_op jit(solution)/shard_map/ppermute | solution.py:465
  58.0 1.5 %collective-permute-start.10 = (bf16[256,512]{1,0:T(8,128)(2,1)S(1)}, bf16[256,512]{1,0:T(8,128)(2,1)S(1)}, u32[]{:S(2)}, u32[]{:S(2)}) collective-permute-start(bf16[256,512]{1,0:T(8,128)(2,1)S(1)} %get-tuple-element.27), channel_id=1, source_target_pairs={{0,1},{1,0},{2,3},{3,2},{4,5},{5,4},{6,7},{7,6},{8,9},{9,8},{10,11... | collective-permute-start | bytes 786440 | tf_op jit(solution)/shard_map/ppermute | solution.py:477

commit v2 on v0

--- a/solution.py
+++ b/solution.py
@@ -1,6 +1,12 @@
+import functools
+
 import jax
 import jax.numpy as jnp
+import ml_dtypes
+import numpy as np
 from jax import lax
+from jax.experimental import pallas as pl
+from jax.experimental.pallas import tpu as pltpu
 from jax.sharding import PartitionSpec as P
 
 BLOCK = 128
@@ -46,7 +52,7 @@
     return jnp.stack(result)
 
 
-def local(images, mask_bits, inv_var, routes, block_slot, kernel_index, coefficients):
+def routed(images, mask_bits, inv_var, routes, block_slot, kernel_index, coefficients):
     peer_count = lax.axis_size("exp")
     held_count = images.shape[2]
     capacity = max(2, 2 * held_count // peer_count)
@@ -131,6 +137,451 @@
     coadded = matched / denominator
     detection = lax.psum(coadded * coadded * denominator, "band")
     return (coadded[None], detection)
+
+
+HALF = TAPS // 2
+EDGE = 32
+REACH = 24
+LINE = 4
+PARTS = 4
+TILE_BLOCKS = BLOCK_ROWS * BLOCK_COLS
+TILE_ROWS = BLOCK_ROWS * BLOCK
+TILE_COLS = BLOCK_COLS * BLOCK
+MEBI = 1024 * 1024
+
+
+def tap_values(offset):
+    span = np.arange(-HALF, HALF + 1, dtype=np.float64)
+    inside = np.abs(offset) <= HALF
+    result = []
+    for spread in kernel_sigmas:
+        total = np.exp(-span * span / (2.0 * spread * spread)).sum()
+        value = np.exp(-offset.astype(np.float64) ** 2 / (2.0 * spread * spread)) / total
+        result.append(np.where(inside, value, 0.0))
+    return np.stack(result)
+
+
+def split_taps(values):
+    high = values.astype(ml_dtypes.bfloat16)
+    low = (values - high.astype(np.float64)).astype(ml_dtypes.bfloat16)
+    return high, low
+
+
+def row_taps(target):
+    values = tap_values(target[:, None] - np.arange(BLOCK)[None, :])
+    return np.concatenate(split_taps(values.reshape(-1, BLOCK)), axis=1)
+
+
+def tap_scales():
+    values = tap_values(np.arange(-HALF, HALF + 1))[:, None, :]
+    factors = np.linspace(1.0, 2.0, 4096, endpoint=False)[None, :, None]
+    rounded = (values * factors).astype(ml_dtypes.bfloat16).astype(np.float64) / factors
+    return factors[0, np.argmin(((rounded - values) ** 2).sum(axis=-1), axis=1), 0]
+
+
+def column_taps():
+    lane = np.arange(BLOCK)
+    beside = np.where(lane < BLOCK // 2, lane + BLOCK, lane - BLOCK)
+    target = np.concatenate([lane, beside])[None, :]
+    values = tap_values(target - lane[:, None]) * tap_scales()[:, None, None]
+    rounded = values.reshape(3 * BLOCK, 2 * BLOCK).astype(ml_dtypes.bfloat16)
+    return np.concatenate([rounded, rounded], axis=0)
+
+
+def code(value):
+    return (value * jnp.abs(value)).astype(jnp.bfloat16)
+
+
+def decode(coded):
+    square = coded.astype(jnp.float32)
+    root = jnp.sqrt(jnp.abs(square))
+    return jnp.where(square < 0, -root, root)
+
+
+def tile_at(place):
+    me = lax.axis_index("exp")
+    return jnp.where(me < LINE // 2, LINE - 1 - place, place)
+
+
+def split_rows(block, mixing):
+    rows = block.shape[0] // 3
+    high, low = [], []
+    for k in range(3):
+        value = mixing[k] * block[k * rows : (k + 1) * rows]
+        rounded = value.astype(jnp.bfloat16)
+        high.append(rounded)
+        low.append((value - rounded.astype(jnp.float32)).astype(jnp.bfloat16))
+    return jnp.concatenate(high + low, axis=1)
+
+
+def spread_columns(target, column, rows, values):
+    beside = values[:, BLOCK:]
+    to_right = lax.broadcasted_iota(jnp.int32, beside.shape, 1) < BLOCK // 2
+    target[column, rows] += values[:, :BLOCK]
+    target[column + 1, rows] += jnp.where(to_right, beside, 0.0)
+    target[column - 1, rows] += jnp.where(to_right, 0.0, beside)
+
+
+def pixel_share(flags, full):
+    part = jnp.where((flags & 1) == 1, 0.5 * full, full)
+    return jnp.where((flags & 6) == 6, 0.0, part)
+
+
+def start_all(pairs, sems):
+    copies = [pltpu.make_async_copy(src, dst, sems.at[n]) for n, (src, dst) in enumerate(pairs)]
+    for copy in copies:
+        copy.start()
+    return copies
+
+
+def in_parts(src, dst, parts):
+    size = src.shape[0] // parts
+    return [(src.at[pl.ds(p * size, size)], dst.at[pl.ds(p * size, size)]) for p in range(parts)]
+
+
+def depth_kernel(held, *refs):
+    routes_in, slots_in, inverse_in, bits_in = refs[:4]
+    out_tiles = refs[4 : 4 + LINE]
+    routes, slots, inverse, bits, depth, sems = refs[4 + LINE :]
+    copies = start_all(
+        [(routes_in, routes), (slots_in, slots), (inverse_in, inverse)] + in_parts(bits_in, bits, PARTS),
+        sems,
+    )
+    depth[...] = jnp.zeros_like(depth)
+    for copy in copies[:3]:
+        copy.wait()
+    for s in range(held):
+        if s % (held // PARTS) == 0:
+            copies[3 + s * PARTS // held].wait()
+        weight = pixel_share(bits[s], inverse[s]).astype(jnp.bfloat16)
+        depth[routes[s] * TILE_BLOCKS + slots[s]] += weight.astype(jnp.float32)
+    for place, ref in enumerate(out_tiles):
+        tile = tile_at(place)
+        for b in range(TILE_BLOCKS):
+            row, col = b // BLOCK_COLS * BLOCK, b % BLOCK_COLS * BLOCK
+            ref[row : row + BLOCK, col : col + BLOCK] = depth[tile * TILE_BLOCKS + b].astype(
+                jnp.bfloat16
+            )
+
+
+def edge_kernel(held, *refs):
+    (
+        routes_in, slots_in, kinds_in, inverse_in, coefs_in, bits_in, images_in, taps_in, col_taps_in, _,
+        weighted, out_edge, _passed,
+        routes, slots, kinds, inverse, coefs, bits, images, taps, col_taps, factors, total, sems,
+    ) = refs
+    strip = lax.axis_index("tile")
+    copies = start_all(
+        [
+            (routes_in, routes), (slots_in, slots), (kinds_in, kinds), (inverse_in, inverse),
+            (coefs_in, coefs), (taps_in, taps), (col_taps_in, col_taps),
+        ]
+        + in_parts(bits_in, bits, PARTS)
+        + in_parts(images_in, images, PARTS),
+        sems,
+    )
+    total[...] = jnp.zeros_like(total)
+    for copy in copies[:6]:
+        copy.wait()
+    scales = tap_scales()
+    for s in range(held):
+        if s % (held // PARTS) == 0:
+            copies[7 + s * PARTS // held].wait()
+            copies[7 + PARTS + s * PARTS // held].wait()
+        share = pixel_share(bits[s], inverse[s])
+        pixels = (share * images[s].astype(jnp.float32)).astype(jnp.bfloat16)
+        weighted[s] = pixels
+        moved = jnp.dot(
+            taps[1 - strip],
+            jnp.concatenate([pixels, pixels], axis=0),
+            preferred_element_type=jnp.float32,
+        )
+        crosses = (slots[s] // BLOCK_COLS == 1 - strip).astype(jnp.float32)
+        factors[s * EDGE : (s + 1) * EDGE] = split_rows(
+            moved, [crosses * coefs[k, kinds[s]] * float(1.0 / scales[k]) for k in range(3)]
+        )
+    copies[6].wait()
+    result = jnp.dot(factors[...], col_taps[...], preferred_element_type=jnp.float32)
+    for s in range(held):
+        column = 1 + routes[s] * BLOCK_COLS + slots[s] % BLOCK_COLS
+        spread_columns(total, column, pl.ds(0, EDGE), result[s * EDGE : (s + 1) * EDGE])
+    for place in range(LINE):
+        for b in range(BLOCK_COLS):
+            out_edge[place, :, b * BLOCK : (b + 1) * BLOCK] = total[
+                1 + tile_at(place) * BLOCK_COLS + b
+            ].astype(jnp.bfloat16)
+
+
+def match_kernel(held, ends, *refs):
+    pl.when(at_end() == ends)(functools.partial(match_tiles, held, *refs))
+
+
+def match_tiles(held, *refs):
+    routes, slots, kinds, coefs, weighted, taps, col_taps = refs[:7]
+    out_tiles = refs[-1 - LINE : -1]
+    total = refs[-1]
+    total[...] = jnp.zeros_like(total)
+    scales = tap_scales()
+    for first in range(0, held, 2):
+        both = jnp.concatenate([weighted[first], weighted[first + 1]], axis=1)
+        moved = jnp.dot(
+            taps[...], jnp.concatenate([both, both], axis=0), preferred_element_type=jnp.float32
+        )
+        for n in range(2):
+            s = first + n
+            slot = slots[s]
+            factors = split_rows(
+                moved[:, n * BLOCK : (n + 1) * BLOCK],
+                [coefs[k, kinds[s]] * float(1.0 / scales[k]) for k in range(3)],
+            )
+            result = jnp.dot(factors, col_taps[...], preferred_element_type=jnp.float32)
+            row = pl.multiple_of(slot // BLOCK_COLS * BLOCK, 8)
+            column = 1 + routes[s] * BLOCK_COLS + slot % BLOCK_COLS
+            spread_columns(total, column, pl.ds(row, BLOCK + 2 * REACH), result)
+    for place in range(LINE):
+        for b in range(BLOCK_COLS):
+            out_tiles[place][:, b * BLOCK : (b + 1) * BLOCK] = total[
+                1 + tile_at(place) * BLOCK_COLS + b, pl.ds(REACH, TILE_ROWS)
+            ]
+
+
+def edge_rows():
+    return pl.ds(pl.multiple_of((1 - lax.axis_index("tile")) * (TILE_ROWS - EDGE), EDGE), EDGE)
+
+
+def relay_kernel(own, got, edge, _after, _, out, _passed):
+    rows = edge_rows()
+    out[...] = code(own[...] + decode(got[...]))
+    out[rows] = code(own[rows] + edge[...].astype(jnp.float32) + decode(got[rows]))
+
+
+def plus_kernel(own, got, *refs):
+    out = refs[-2]
+    out[...] = (own[...].astype(jnp.float32) + got[...].astype(jnp.float32)).astype(jnp.bfloat16)
+
+
+def at_end():
+    me = lax.axis_index("exp")
+    return jnp.logical_or(me == 0, me == LINE - 1)
+
+
+def turn_kernel(third, last, got, _, out, _passed):
+    @pl.when(at_end())
+    def _():
+        out[...] = third[...]
+
+    @pl.when(jnp.logical_not(at_end()))
+    def _():
+        out[...] = (last[...].astype(jnp.float32) + got[...].astype(jnp.float32)).astype(jnp.bfloat16)
+
+
+def gather_kernel(
+    third_d, last_d, got_d, got_mid_d, third_m, last_m, edge, got_m, out_sum, out_depth, out_inverse
+):
+    end = at_end()
+    rows = edge_rows()
+    out_sum[...] = jnp.where(end, last_m[...], third_m[...] + decode(got_m[...]))
+    out_sum[rows] += jnp.where(end, edge[3].astype(jnp.float32), edge[2].astype(jnp.float32))
+    own_d = jnp.where(end, last_d[...].astype(jnp.float32), third_d[...].astype(jnp.float32))
+    denominator = (1.0 + own_d) + got_d[...].astype(jnp.float32) + got_mid_d[...].astype(jnp.float32)
+    out_depth[...] = denominator
+    out_inverse[...] = 1.0 / denominator
+
+
+def coadded(matched, inverse, got_mid_m, got_last_m):
+    return (matched[...] + decode(jnp.where(at_end(), got_last_m[...], got_mid_m[...]))) * inverse[...]
+
+
+def term_kernel(matched, depth, inverse, got_mid_m, got_last_m, out_term):
+    coadd = coadded(matched, inverse, got_mid_m, got_last_m)
+    out_term[...] = (coadd * coadd * depth[...]).astype(jnp.bfloat16)
+
+
+def coadd_kernel(matched, inverse, got_mid_m, got_last_m, out_coadd):
+    out_coadd[...] = coadded(matched, inverse, got_mid_m, got_last_m)
+
+
+def first_kernel(tile_0, tile_1, tile_2, edge, far, next_far, third):
+    rows = edge_rows()
+    for place, (source, out) in enumerate(((tile_0, far), (tile_1, next_far), (tile_2, third))):
+        out[...] = code(source[...])
+        out[rows] = code(source[rows] + edge[place].astype(jnp.float32))
+
+
+def in_vmem(count):
+    return [pl.BlockSpec(memory_space=pltpu.VMEM)] * count
+
+
+def in_smem(count):
+    return [pl.BlockSpec(memory_space=pltpu.SMEM)] * count
+
+
+def in_hbm(count):
+    return [pl.BlockSpec(memory_space=pltpu.HBM)] * count
+
+
+def vmem_limit(mebibytes):
+    return pltpu.CompilerParams(vmem_limit_bytes=mebibytes * MEBI)
+
+
+def work(microseconds):
+    return pl.CostEstimate(
+        flops=microseconds * 1_150_000_000, bytes_accessed=0, transcendentals=0
+    )
+
+
+def reduced(images, mask_bits, inv_var, routes, block_slot, kernel_index, coefficients):
+    held = images.shape[2]
+    tile = jax.ShapeDtypeStruct((TILE_ROWS, TILE_COLS), jnp.bfloat16)
+    wide = jax.ShapeDtypeStruct((TILE_ROWS, TILE_COLS), jnp.float32)
+    columns = LINE * BLOCK_COLS + 2
+    target, slot, kind = routes.reshape(held), block_slot.reshape(held), kernel_index.reshape(held)
+    mixing = coefficients.T
+    in_place = [pl.BlockSpec(memory_space=pl.ANY)]
+    beside = [(0, 1), (1, 0), (2, 3), (3, 2)]
+    across = [(1, 2), (2, 1)]
+
+    scalars = [pltpu.SMEM((held,), kind) for kind in (jnp.int32, jnp.int32, jnp.float32)]
+    blocks = jax.ShapeDtypeStruct((held, BLOCK, BLOCK), jnp.bfloat16)
+    far_d, next_d, third_d, last_d = pl.pallas_call(
+        functools.partial(depth_kernel, held),
+        out_shape=[tile] * LINE,
+        in_specs=in_hbm(4),
+        out_specs=in_vmem(LINE),
+        scratch_shapes=scalars
+        + [
+            pltpu.VMEM((held, BLOCK, BLOCK), jnp.int32),
+            pltpu.VMEM((LINE * TILE_BLOCKS, BLOCK, BLOCK), jnp.float32),
+            pltpu.SemaphoreType.DMA((3 + PARTS,)),
+        ],
+        compiler_params=vmem_limit(56),
+        cost_estimate=work(2),
+        name="depth",
+    )(target, slot, inv_var.reshape(held), mask_bits[0, 0])
+    got_far_d = lax.ppermute(far_d, "exp", [(0, 1), (LINE - 1, LINE - 2)])
+
+    edge_taps = np.stack([row_taps(np.arange(-EDGE, 0)), row_taps(np.arange(BLOCK, BLOCK + EDGE))])
+    col_taps = jnp.asarray(column_taps())
+    weighted, edge, next_d = pl.pallas_call(
+        functools.partial(edge_kernel, held),
+        out_shape=[blocks, jax.ShapeDtypeStruct((LINE, EDGE, TILE_COLS), jnp.bfloat16), tile],
+        in_specs=in_hbm(9) + in_place,
+        out_specs=in_vmem(2) + in_place,
+        input_output_aliases={9: 2},
+        scratch_shapes=[pltpu.SMEM((held,), jnp.int32)]
+        + scalars
+        + [
+            pltpu.SMEM(mixing.shape, jnp.float32),
+            pltpu.VMEM((held, BLOCK, BLOCK), jnp.int32),
+            pltpu.VMEM((held, BLOCK, BLOCK), jnp.bfloat16),
+            pltpu.VMEM(edge_taps.shape, jnp.bfloat16),
+            pltpu.VMEM(col_taps.shape, jnp.bfloat16),
+            pltpu.VMEM((held * EDGE, 6 * BLOCK), jnp.bfloat16),
+            pltpu.VMEM((columns, EDGE, BLOCK), jnp.float32),
+            pltpu.SemaphoreType.DMA((7 + 2 * PARTS,)),
+        ],
+        compiler_params=vmem_limit(24),
+        cost_estimate=work(3),
+        name="edges",
+    )(
+        target, slot, kind, inv_var.reshape(held), mixing, mask_bits[0, 0], images[0, 0],
+        jnp.asarray(edge_taps), col_taps, next_d,
+    )
+    other_edge = lax.ppermute(edge, "tile", [(0, 1), (1, 0)])
+    got_next_d = lax.ppermute(next_d, "exp", [(0, 1), (LINE - 1, LINE - 2)])
+    own_rows = jnp.asarray(row_taps(np.arange(-REACH, BLOCK + REACH)))
+
+    def match(ends, after):
+        return pl.pallas_call(
+            functools.partial(match_kernel, held, ends),
+            out_shape=[wide] * LINE,
+            in_specs=in_smem(4) + in_vmem(3) + in_place * len(after),
+            out_specs=in_vmem(LINE),
+            scratch_shapes=[pltpu.VMEM((columns, TILE_ROWS + 2 * REACH, BLOCK), jnp.float32)],
+            compiler_params=vmem_limit(24),
+            cost_estimate=work(0),
+            name="match",
+        )(target, slot, kind, mixing, weighted, own_rows, col_taps, *after)
+
+    end_tiles = match(True, [])
+    far_m, next_m, third_m = pl.pallas_call(
+        first_kernel,
+        out_shape=[tile, tile, tile],
+        in_specs=in_vmem(4),
+        out_specs=in_vmem(3),
+        compiler_params=vmem_limit(24),
+        cost_estimate=work(0),
+        name="first",
+    )(*end_tiles[:3], other_edge)
+
+    def passing(kernel, name, operands, after, passed):
+        return pl.pallas_call(
+            kernel,
+            out_shape=[tile, jax.ShapeDtypeStruct(passed.shape, passed.dtype)],
+            in_specs=in_vmem(len(operands)) + in_place * (len(after) + 1),
+            out_specs=in_vmem(1) + in_place,
+            input_output_aliases={len(operands) + len(after): 1},
+            compiler_params=vmem_limit(24),
+            cost_estimate=work(1),
+            name=name,
+        )(*operands, *after, passed)
+
+    got_far_m = lax.ppermute(far_m, "exp", [(0, 1), (LINE - 1, LINE - 2)])
+    far_sum, next_m = passing(plus_kernel, "plus", [far_d, got_far_d], [], next_m)
+    mid_far_d = lax.ppermute(far_sum, "exp", across)
+    mid_tiles = match(False, [far_sum])
+    next_sum, next_m = passing(plus_kernel, "plus", [next_d, got_next_d], [mid_tiles[0]], next_m)
+    got_next_m = lax.ppermute(next_m, "exp", beside)
+    mid_d = lax.ppermute(next_sum, "exp", across)
+    far_relayed, third_m = passing(
+        relay_kernel, "relay", [mid_tiles[0], got_far_m, other_edge[0]], [mid_far_d], third_m
+    )
+    mid_far_m = lax.ppermute(far_relayed, "exp", across)
+    turned, third_m = passing(turn_kernel, "turn", [third_d, last_d, mid_far_d], [], third_m)
+    got_d = lax.ppermute(turned, "exp", beside)
+    next_relayed, third_m = passing(
+        relay_kernel, "relay", [mid_tiles[1], got_next_m, other_edge[1]], [mid_d], third_m
+    )
+    mid_m = lax.ppermute(next_relayed, "exp", across)
+    got_m = lax.ppermute(third_m, "exp", [(0, 1), (LINE - 1, LINE - 2)])
+    last_relayed, _ = passing(
+        relay_kernel, "relay", [mid_tiles[3], mid_far_m, other_edge[3]], [got_d], jnp.zeros((8, 128), jnp.float32)
+    )
+    end_m = lax.ppermute(last_relayed, "exp", [(1, 0), (LINE - 2, LINE - 1)])
+    matched, depth, inverse = pl.pallas_call(
+        gather_kernel,
+        out_shape=[wide] * 3,
+        in_specs=in_vmem(8),
+        out_specs=in_vmem(3),
+        compiler_params=vmem_limit(24),
+        cost_estimate=work(1),
+        name="gather",
+    )(third_d, last_d, got_d, mid_d, mid_tiles[2], end_tiles[3], other_edge, got_m)
+
+    def ending(kernel, name, shape, *operands):
+        return pl.pallas_call(
+            kernel,
+            out_shape=shape,
+            in_specs=in_vmem(len(operands)),
+            out_specs=pl.BlockSpec(memory_space=pltpu.VMEM),
+            compiler_params=vmem_limit(24),
+            cost_estimate=work(1),
+            name=name,
+        )(*operands)
+
+    term = ending(term_kernel, "term", tile, matched, depth, inverse, mid_m, end_m)
+    coadd = ending(coadd_kernel, "coadd", wide, matched, inverse, mid_m, end_m)
+    other_term = lax.ppermute(term, "band", [(0, 1), (1, 0)])
+    detection = term.astype(jnp.float32) + other_term.astype(jnp.float32)
+    return (coadd[None], detection)
+
+
+def local(images, mask_bits, inv_var, routes, block_slot, kernel_index, coefficients):
+    peers = lax.axis_size("exp")
+    partial_sums_fit = peers * TILE_BLOCKS <= 2 * images.shape[2]
+    pairs = lax.axis_size("tile") == 2 and lax.axis_size("band") == 2
+    plan = reduced if partial_sums_fit and pairs and peers == LINE else routed
+    return plan(images, mask_bits, inv_var, routes, block_slot, kernel_index, coefficients)
 
 
 def solution(mesh):

time: 138 us -> 52.7 us (0.38)
  waiting for transfers between devices: 58 us -> 12.3 us
  matrix products: 17 us -> 0 us
  other arithmetic: 15.7 us -> 0.87 us
  Pallas kernels: 0 us -> 13.8 us
  between operations: 14.2 us -> 0.98 us
  starting transfers between devices: 27.8 us -> 22.9 us
  local copies, waits for them, and re-layouts: 4.37 us -> 1.37 us
    psum x1 -> x0, waiting for transfers between devices: 24.8 us -> none  [local(): detection = lax.psum(coadded * coadded * denominator, 'band')]
    all_to_all x3 -> x0, waiting for transfers between devices: 17.2 us -> none  [the longest x1 16.2 us: local(): lax.all_to_all(send_weighted, 'exp', split_axis=0, concat_axis=0, tiled=T...]
    dot_general x7 -> x0, matrix products: 17 us -> none  [the longest x1 6.67 us: local(): jnp.einsum('kyp,kpc->kyc', framed, column_mix, precision=lax.Precision.HI...]
    all_to_all x3 -> x0, starting transfers between devices: 14.6 us -> none  [the longest x1 6.32 us: local(): lax.all_to_all(labels, 'exp', split_axis=0, concat_axis=0, tiled=True)]
    pallas_call x0 -> x14, Pallas kernels: none -> 13.8 us  [the longest x2 4.48 us: match(): pl.pallas_call(functools.partial(match_kernel, held, ends), out_shape=[wi...]
    ppermute x4 -> x13, starting transfers between devices: 13.2 us -> 22.9 us  [the longest x1 5.71 us: reduced(): got_next_m = lax.ppermute(next_m, 'exp', beside)]
    div x4 -> x0, other arithmetic: 8.28 us -> none  [band_matrix(): jnp.where(inside, jnp.exp(-offset * offset / (2.0 * spread * spread)), 0.0)]
    ppermute x4 -> x13, waiting for transfers between devices: 16.1 us -> 12.3 us  [the longest x1 5.34 us: reduced(): got_next_m = lax.ppermute(next_m, 'exp', beside)]
  transfers between devices with their start and end apart: 8 -> 13, of which waited for: 5 -> 5; matrix products, arithmetic and copies ran while one was open for 16% -> 0% of each run, Pallas kernels for 0% -> 21%
where the time goes in v2:
time: 52.7 us; the launch traced here: 52.3 us
  starting transfers between devices  22.9 us (43%)
  Pallas kernels  13.8 us (26%)
  waiting for transfers between devices  12.3 us (23%)
  local copies, waits for them, and re-layouts  1.37 us (3%)
  between operations  0.98 us (2%)
  other arithmetic  0.87 us (2%)
    ppermute x1, starting transfers between devices, reduced(): got_next_m = lax.ppermute(next_m, 'exp', beside)  5.71 us
    ppermute x1, waiting for transfers between devices, reduced(): got_next_m = lax.ppermute(next_m, 'exp', beside)  5.34 us
    ppermute x1, starting transfers between devices, reduced(): got_far_d = lax.ppermute(far_d, 'exp', [(0, 1), (LINE - 1, LINE - 2)])  4.94 us
    ppermute x1, waiting for transfers between devices, reduced(): end_m = lax.ppermute(last_relayed, 'exp', [(1, 0), (LINE - 2, LINE - 1)])  4.92 us
    pallas_call x2, Pallas kernels, match(): pl.pallas_call(functools.partial(match_kernel, held, ends), out_shape=[wi...  4.48 us
    ppermute x1, starting transfers between devices, reduced(): got_m = lax.ppermute(third_m, 'exp', [(0, 1), (LINE - 1, LINE - 2)])  3.94 us
    pallas_call x1, Pallas kernels, reduced(): pl.pallas_call(functools.partial(edge_kernel, held), out_shape=[blocks, j...  2.65 us
    pallas_call x1, Pallas kernels, reduced(): pl.pallas_call(functools.partial(depth_kernel, held), out_shape=[tile] *...  2.47 us
  transfers between devices with their start and end apart: 13, of which 5 were waited for; matrix products, arithmetic and copies ran while one was open for 0% of the time, Pallas kernels for 21%

profile of v2, /device:TPU:0, one launch (start us, length us, event | category | flops | bytes accessed | tf_op | source)
XLA Modules:
  0.0 52.3 jit_solution(5036534825962646835)
XLA Ops:
  0.7 2.5 %depth.1 = (bf16[256,512]{1,0:T(8,128)(2,1)}, bf16[256,512]{1,0:T(8,128)(2,1)}, bf16[256,512]{1,0:T(8,128)(2,1)}, bf16[256,512]{1,0:T(8,128)(2,1)}) custom-call(s32[16]{0:T(128)} %bitcast.17, s32[16]{0:T(128)} %bitcast.21, f32[16]{0:T(128)} %bitcast.31, s32[16,128,128]{2,1,0:T(8,128)} %bitcast.28), custom_call_target="tpu_custom_call" | custom-call | flops 2300000000 | tf_op jit(solution)/shard_map/depth/pallas_call | solution.py:446
  3.2 4.9 %collective-permute-start = (bf16[256,512]{1,0:T(8,128)(2,1)}, bf16[256,512]{1,0:T(8,128)(2,1)S(1)}, u32[]{:S(2)}, u32[]{:S(2)}) collective-permute-start(bf16[256,512]{1,0:T(8,128)(2,1)} %get-tuple-element.36.own), channel_id=1, source_target_pairs={{0,4},{12,8},{1,5},{13,9},{2,6},{14,10},{3,7},{15,11},{16,20},{28,... | collective-permute-start | bytes 786440 | tf_op jit(solution)/shard_map/ppermute | solution.py:461
  8.2 0.6 %copy-done.2 = f32[64,3]{0,1:T(4,128)S(1)} copy-done((f32[64,3]{0,1:T(4,128)S(1)}, f32[64,3]{0,1:T(4,128)}, u32[]{:S(2)}) %copy-start.2) | copy-done | bytes 792
  8.8 2.7 %edges.1 = (bf16[16,128,128]{2,1,0:T(8,128)(2,1)S(1)}, bf16[4,32,512]{2,1,0:T(8,128)(2,1)S(1)}, bf16[256,512]{1,0:T(8,128)(2,1)}) custom-call(s32[16]{0:T(128)S(1)} %bitcast.18, s32[16]{0:T(128)S(1)} %bitcast.22, s32[16]{0:T(128)S(1)} %bitcast.25, f32[16]{0:T(128)S(1)} %bitcast.32, f32[3,64]{1,0:T(4,128)S(1)} %bitcast.14, ...), custom_call_target="tpu_custom_call", output_to_operand_aliasing={{2}: (9, {})} | custom-call | flops 3449999872 | tf_op jit(solution)/shard_map/edges/pallas_call | solution.py:465
  11.5 1.6 %collective-permute-start.1 = (bf16[4,32,512]{2,1,0:T(8,128)(2,1)S(1)}, bf16[4,32,512]{2,1,0:T(8,128)(2,1)S(1)}, u32[]{:S(2)}, u32[]{:S(2)}) collective-permute-start(bf16[4,32,512]{2,1,0:T(8,128)(2,1)S(1)} %get-tuple-element.42), channel_id=1, source_target_pairs={{0,2},{2,0},{1,3},{3,1},{4,6},{6,4},{5,7},{7,5},{8,10},{10,8},{9,1... | collective-permute-start | bytes 393224 | tf_op jit(solution)/shard_map/ppermute | solution.py:490
  13.0 1.3 %collective-permute-start.5 = (bf16[256,512]{1,0:T(8,128)(2,1)}, bf16[256,512]{1,0:T(8,128)(2,1)S(1)}, u32[]{:S(2)}, u32[]{:S(2)}) collective-permute-start(bf16[256,512]{1,0:T(8,128)(2,1)} %get-tuple-element.50.own), channel_id=1, source_target_pairs={{0,4},{12,8},{1,5},{13,9},{2,6},{14,10},{3,7},{15,11},{16,20},{28,... | collective-permute-start | bytes 786440 | tf_op jit(solution)/shard_map/ppermute | solution.py:491
  14.3 3.9 %match.2 = (f32[256,512]{1,0:T(8,128)S(1)}, f32[256,512]{1,0:T(8,128)S(1)}, f32[256,512]{1,0:T(8,128)S(1)}, f32[256,512]{1,0:T(8,128)S(1)}) custom-call(s32[16]{0:T(128)S(1)} %bitcast.19, s32[16]{0:T(128)S(1)} %bitcast.23, s32[16]{0:T(128)S(1)} %bitcast.26, f32[3,64]{1,0:T(4,128)S(1)} %bitcast.15, bf16[16,128,128]{2,1,0:T(8,128)(2,1)S(1)} %get-tuple-element.38.refs_4_, ...), custom_call_target="tpu_custom_call" | custom-call | tf_op jit(solution)/shard_map/match/pallas_call | solution.py:495
  18.3 0.2 first.1
  18.4 1.3 %collective-permute-start.3 = (bf16[256,512]{1,0:T(8,128)(2,1)S(1)}, bf16[256,512]{1,0:T(8,128)(2,1)S(1)}, u32[]{:S(2)}, u32[]{:S(2)}) collective-permute-start(bf16[256,512]{1,0:T(8,128)(2,1)S(1)} %get-tuple-element.46), channel_id=1, source_target_pairs={{0,4},{12,8},{1,5},{13,9},{2,6},{14,10},{3,7},{15,11},{16,20},{28,... | collective-permute-start | bytes 786440 | tf_op jit(solution)/shard_map/ppermute | solution.py:529
  19.8 0.7 %collective-permute-start.2 = (bf16[256,512]{1,0:T(8,128)(2,1)S(1)}, bf16[256,512]{1,0:T(8,128)(2,1)S(1)}, u32[]{:S(2)}, u32[]{:S(2)}) collective-permute-start(bf16[256,512]{1,0:T(8,128)(2,1)S(1)} %get-tuple-element.44.refs_7_), channel_id=1, source_target_pairs={{4,8},{8,4},{5,9},{9,5},{6,10},{10,6},{7,11},{11,7},{20,24},{24,20... | collective-permute-start | bytes 786440 | tf_op jit(solution)/shard_map/ppermute | solution.py:531
  20.5 0.6 %match.3 = (f32[256,512]{1,0:T(8,128)S(1)}, f32[256,512]{1,0:T(8,128)S(1)}, f32[256,512]{1,0:T(8,128)S(1)}, f32[256,512]{1,0:T(8,128)S(1)}) custom-call(s32[16]{0:T(128)S(1)} %bitcast.20, s32[16]{0:T(128)S(1)} %bitcast.24, s32[16]{0:T(128)S(1)} %bitcast.27, f32[3,64]{1,0:T(4,128)S(1)} %bitcast.16, bf16[16,128,128]{2,1,0:T(8,128)(2,1)S(1)} %get-tuple-element.38.refs_4_, ...), custom_call_target="tpu_custom_call" | custom-call | tf_op jit(solution)/shard_map/match/pallas_call | solution.py:495
  21.2 1.0 %plus.3 = (bf16[256,512]{1,0:T(8,128)(2,1)S(1)}, bf16[256,512]{1,0:T(8,128)(2,1)S(1)}) custom-call(bf16[256,512]{1,0:T(8,128)(2,1)} %get-tuple-element.50.own, bf16[256,512]{1,0:T(8,128)(2,1)S(1)} %collective-permute-done.5.got, f32[256,512]{1,0:T(8,128)S(1)} %get-tuple-element.45.own.refs_0_, ...), custom_call_target="tpu_custom_call", output_to_operand_aliasing={{1}: (3, {})} | custom-call | flops 1150000000 | tf_op jit(solution)/shard_map/plus/pallas_call | solution.py:518
  22.2 0.7 %collective-permute-start.6 = (bf16[256,512]{1,0:T(8,128)(2,1)S(1)}, bf16[256,512]{1,0:T(8,128)(2,1)S(1)}, u32[]{:S(2)}, u32[]{:S(2)}) collective-permute-start(bf16[256,512]{1,0:T(8,128)(2,1)S(1)} %get-tuple-element.52), channel_id=1, source_target_pairs={{4,8},{8,4},{5,9},{9,5},{6,10},{10,6},{7,11},{11,7},{20,24},{24,20... | collective-permute-start | bytes 786440 | tf_op jit(solution)/shard_map/ppermute | solution.py:535
  22.9 5.7 %collective-permute-start.7 = (bf16[256,512]{1,0:T(8,128)(2,1)S(1)}, bf16[256,512]{1,0:T(8,128)(2,1)S(1)}, u32[]{:S(2)}, u32[]{:S(2)}) collective-permute-start(bf16[256,512]{1,0:T(8,128)(2,1)S(1)} %get-tuple-element.56), channel_id=1, source_target_pairs={{0,4},{4,0},{8,12},{12,8},{1,5},{5,1},{9,13},{13,9},{2,6},{6,2},{1... | collective-permute-start | bytes 786440 | tf_op jit(solution)/shard_map/ppermute | solution.py:534
  28.6 0.3 relay.3
  28.9 0.6 %copy-done.11 = bf16[256,512]{1,0:T(8,128)(2,1)S(1)} copy-done((bf16[256,512]{1,0:T(8,128)(2,1)S(1)}, bf16[256,512]{1,0:T(8,128)(2,1)}, u32[]{:S(2)}) %copy-start.11) | copy-done | bytes 262168
  29.6 0.1 collective-permute-start.4
  29.8 0.7 %collective-permute-start.10 = (bf16[256,512]{1,0:T(8,128)(2,1)S(1)}, bf16[256,512]{1,0:T(8,128)(2,1)S(1)}, u32[]{:S(2)}, u32[]{:S(2)}) collective-permute-start(bf16[256,512]{1,0:T(8,128)(2,1)S(1)} %get-tuple-element.63), channel_id=1, source_target_pairs={{4,8},{8,4},{5,9},{9,5},{6,10},{10,6},{7,11},{11,7},{20,24},{24,20... | collective-permute-start | bytes 786440 | tf_op jit(solution)/shard_map/ppermute | solution.py:539
  30.5 5.3 %collective-permute-done.7.got = bf16[256,512]{1,0:T(8,128)(2,1)S(1)} collective-permute-done((bf16[256,512]{1,0:T(8,128)(2,1)S(1)}, bf16[256,512]{1,0:T(8,128)(2,1)S(1)}, u32[]{:S(2)}, u32[]{:S(2)}) %collective-permute-start.7) | collective-permute-done | bytes 262176 | tf_op jit(solution)/shard_map/ppermute | solution.py:534
  35.8 0.3 relay.4
  36.1 3.9 %collective-permute-start.8 = (bf16[256,512]{1,0:T(8,128)(2,1)S(1)}, bf16[256,512]{1,0:T(8,128)(2,1)S(1)}, u32[]{:S(2)}, u32[]{:S(2)}) collective-permute-start(bf16[256,512]{1,0:T(8,128)(2,1)S(1)} %get-tuple-element.58), channel_id=1, source_target_pairs={{0,4},{12,8},{1,5},{13,9},{2,6},{14,10},{3,7},{15,11},{16,20},{28,... | collective-permute-start | bytes 786440 | tf_op jit(solution)/shard_map/ppermute | solution.py:546
  40.1 0.7 %collective-permute-start.9 = (bf16[256,512]{1,0:T(8,128)(2,1)S(1)}, bf16[256,512]{1,0:T(8,128)(2,1)S(1)}, u32[]{:S(2)}, u32[]{:S(2)}) collective-permute-start(bf16[256,512]{1,0:T(8,128)(2,1)S(1)} %get-tuple-element.61), channel_id=1, source_target_pairs={{4,8},{8,4},{5,9},{9,5},{6,10},{10,6},{7,11},{11,7},{20,24},{24,20... | collective-permute-start | bytes 786440 | tf_op jit(solution)/shard_map/ppermute | solution.py:545
  40.7 0.2 collective-permute-done.4.got_d._after
  41.0 0.3 relay.5
  41.3 1.3 %collective-permute-start.11 = (bf16[256,512]{1,0:T(8,128)(2,1)S(1)}, bf16[256,512]{1,0:T(8,128)(2,1)S(1)}, u32[]{:S(2)}, u32[]{:S(2)}) collective-permute-start(bf16[256,512]{1,0:T(8,128)(2,1)S(1)} %get-tuple-element.64), channel_id=1, source_target_pairs={{4,0},{8,12},{5,1},{9,13},{6,2},{10,14},{7,3},{11,15},{20,16},{24,... | collective-permute-start | bytes 786440 | tf_op jit(solution)/shard_map/ppermute | solution.py:550
  42.6 1.4 %collective-permute-done.8.got_m = bf16[256,512]{1,0:T(8,128)(2,1)S(1)} collective-permute-done((bf16[256,512]{1,0:T(8,128)(2,1)S(1)}, bf16[256,512]{1,0:T(8,128)(2,1)S(1)}, u32[]{:S(2)}, u32[]{:S(2)}) %collective-permute-start.8) | collective-permute-done | bytes 262176 | tf_op jit(solution)/shard_map/ppermute | solution.py:546
  43.9 0.7 %gather.1 = (f32[256,512]{1,0:T(8,128)S(1)}, f32[256,512]{1,0:T(8,128)S(1)}, f32[256,512]{1,0:T(8,128)S(1)}) custom-call(bf16[256,512]{1,0:T(8,128)(2,1)S(1)} %copy-done.11, bf16[256,512]{1,0:T(8,128)(2,1)S(1)} %copy-done.12, bf16[256,512]{1,0:T(8,128)(2,1)S(1)} %collective-permute-done.4.got_d._after, ...), custom_call_target="tpu_custom_call" | custom-call | flops 1150000000 | tf_op jit(solution)/shard_map/gather/pallas_call | solution.py:551
  44.6 4.9 %collective-permute-done.11.got_last_m = bf16[256,512]{1,0:T(8,128)(2,1)S(1)} collective-permute-done((bf16[256,512]{1,0:T(8,128)(2,1)S(1)}, bf16[256,512]{1,0:T(8,128)(2,1)S(1)}, u32[]{:S(2)}, u32[]{:S(2)}) %collective-permute-start.11) | collective-permute-done | bytes 262176 | tf_op jit(solution)/shard_map/ppermute | solution.py:550
  49.5 0.3 term.1
  49.9 1.1 %coadd.1 = f32[256,512]{1,0:T(8,128)} custom-call(f32[256,512]{1,0:T(8,128)S(1)} %get-tuple-element.59.matched, f32[256,512]{1,0:T(8,128)S(1)} %get-tuple-element.60.inverse, bf16[256,512]{1,0:T(8,128)(2,1)S(1)} %collective-permute-done.9.got_mid_m, bf16[256,512]{1,0:T(8,128)(2,1)S(1)} %collective-permute-done.11.got_last_m), custom_call_target="tpu_custom_call" | custom-call | flops 1150000000 | tf_op jit(solution)/shard_map/coadd/pallas_call | solution.py:562
  51.0 0.5 collective-permute-done.12
  51.4 0.9 %convert_add_fusion = f32[256,512]{1,0:T(8,128)} fusion(bf16[256,512]{1,0:T(8,128)(2,1)S(1)} %collective-permute-done.12, bf16[256,512]{1,0:T(8,128)(2,1)S(1)} %term.1), kind=kLoop, calls=%fused_computation | loop fusion | flops 393216 | bytes 1048576 | tf_op jit(solution)/shard_map/add | solution.py:575
  (37 shorter events, 0.3 us)
Async XLA Ops:
  0.6 7.5 %copy-start = (bf16[768,256]{1,0:T(8,128)(2,1)S(1)}, bf16[768,256]{1,0:T(8,128)(2,1)}, u32[]{:S(2)}) copy-start(bf16[768,256]{1,0:T(8,128)(2,1)} %constant.8.clone.refs_8_.refs_6_) | copy-start | bytes 1179652
  0.6 7.5 %copy-start.6 = (s32[1,1,16,128,128]{4,3,2,1,0:T(8,128)S(1)}, s32[1,1,16,128,128]{4,3,2,1,0:T(8,128)}, u32[]{:S(2)}) copy-start(s32[1,1,16,128,128]{4,3,2,1,0:T(8,128)} %param.11) | copy-start | bytes 3145732
  0.7 7.5 %copy-start.7 = (bf16[1,1,16,128,128]{4,3,2,1,0:T(8,128)(2,1)S(1)}, bf16[1,1,16,128,128]{4,3,2,1,0:T(8,128)(2,1)}, u32[]{:S(2)}) copy-start(bf16[1,1,16,128,128]{4,3,2,1,0:T(8,128)(2,1)} %param.10) | copy-start | bytes 1572868
  0.7 7.5 %copy-start.9 = (f32[1,1,16]{2,1,0:T(1,128)S(1)}, f32[1,1,16]{2,1,0:T(1,128)}, u32[]{:S(2)}) copy-start(f32[1,1,16]{2,1,0:T(1,128)} %param.12) | copy-start | bytes 196
  0.7 7.5 %copy-start.10 = (bf16[2,96,256]{2,1,0:T(8,128)(2,1)S(1)}, bf16[2,96,256]{2,1,0:T(8,128)(2,1)}, u32[]{:S(2)}) copy-start(bf16[2,96,256]{2,1,0:T(8,128)(2,1)} %constant.9.clone.refs_7_) | copy-start | bytes 294916
  3.2 16.6 %collective-permute-start = (bf16[256,512]{1,0:T(8,128)(2,1)}, bf16[256,512]{1,0:T(8,128)(2,1)S(1)}, u32[]{:S(2)}, u32[]{:S(2)}) collective-permute-start(bf16[256,512]{1,0:T(8,128)(2,1)} %get-tuple-element.36.own), channel_id=1, source_target_pairs={{0,4},{12,8},{1,5},{13,9},{2,6},{14,10},{3,7},{15,11},{16,20},{28,... | collective-permute-start | bytes 786440 | tf_op jit(solution)/shard_map/ppermute | solution.py:461
  8.1 0.7 %copy-start.2 = (f32[64,3]{0,1:T(4,128)S(1)}, f32[64,3]{0,1:T(4,128)}, u32[]{:S(2)}) copy-start(f32[64,3]{0,1:T(4,128)} %param.16) | copy-start | bytes 2308
  8.1 0.7 %copy-start.3 = (s32[1,1,16,1]{2,3,1,0:T(1,128)S(1)}, s32[1,1,16,1]{2,3,1,0:T(1,128)}, u32[]{:S(2)}) copy-start(s32[1,1,16,1]{2,3,1,0:T(1,128)} %param.13) | copy-start | bytes 196
  8.1 0.7 %copy-start.4 = (s32[1,1,16]{2,1,0:T(1,128)S(1)}, s32[1,1,16]{2,1,0:T(1,128)}, u32[]{:S(2)}) copy-start(s32[1,1,16]{2,1,0:T(1,128)} %param.14) | copy-start | bytes 196
  8.2 0.7 %copy-start.5 = (s32[1,1,16]{2,1,0:T(1,128)S(1)}, s32[1,1,16]{2,1,0:T(1,128)}, u32[]{:S(2)}) copy-start(s32[1,1,16]{2,1,0:T(1,128)} %param.15) | copy-start | bytes 196
  8.8 5.5 %copy-start.1 = (bf16[528,256]{1,0:T(8,128)(2,1)S(1)}, bf16[528,256]{1,0:T(8,128)(2,1)}, u32[]{:S(2)}) copy-start(bf16[528,256]{1,0:T(8,128)(2,1)} %constant.10.clone.refs_5_) | copy-start | bytes 811012
  11.5 6.8 %collective-permute-start.1 = (bf16[4,32,512]{2,1,0:T(8,128)(2,1)S(1)}, bf16[4,32,512]{2,1,0:T(8,128)(2,1)S(1)}, u32[]{:S(2)}, u32[]{:S(2)}) collective-permute-start(bf16[4,32,512]{2,1,0:T(8,128)(2,1)S(1)} %get-tuple-element.42), channel_id=1, source_target_pairs={{0,2},{2,0},{1,3},{3,1},{4,6},{6,4},{5,7},{7,5},{8,10},{10,8},{9,1... | collective-permute-start | bytes 393224 | tf_op jit(solution)/shard_map/ppermute | solution.py:490
  13.0 8.1 %collective-permute-start.5 = (bf16[256,512]{1,0:T(8,128)(2,1)}, bf16[256,512]{1,0:T(8,128)(2,1)S(1)}, u32[]{:S(2)}, u32[]{:S(2)}) collective-permute-start(bf16[256,512]{1,0:T(8,128)(2,1)} %get-tuple-element.50.own), channel_id=1, source_target_pairs={{0,4},{12,8},{1,5},{13,9},{2,6},{14,10},{3,7},{15,11},{16,20},{28,... | collective-permute-start | bytes 786440 | tf_op jit(solution)/shard_map/ppermute | solution.py:491
  18.2 1.5 %copy-start.8 = (bf16[256,512]{1,0:T(8,128)(2,1)S(1)}, bf16[256,512]{1,0:T(8,128)(2,1)}, u32[]{:S(2)}) copy-start(bf16[256,512]{1,0:T(8,128)(2,1)} %get-tuple-element.36.own) | copy-start | bytes 786436
  18.4 10.1 %collective-permute-start.3 = (bf16[256,512]{1,0:T(8,128)(2,1)S(1)}, bf16[256,512]{1,0:T(8,128)(2,1)S(1)}, u32[]{:S(2)}, u32[]{:S(2)}) collective-permute-start(bf16[256,512]{1,0:T(8,128)(2,1)S(1)} %get-tuple-element.46), channel_id=1, source_target_pairs={{0,4},{12,8},{1,5},{13,9},{2,6},{14,10},{3,7},{15,11},{16,20},{28,... | collective-permute-start | bytes 786440 | tf_op jit(solution)/shard_map/ppermute | solution.py:529
  19.8 8.7 %collective-permute-start.2 = (bf16[256,512]{1,0:T(8,128)(2,1)S(1)}, bf16[256,512]{1,0:T(8,128)(2,1)S(1)}, u32[]{:S(2)}, u32[]{:S(2)}) collective-permute-start(bf16[256,512]{1,0:T(8,128)(2,1)S(1)} %get-tuple-element.44.refs_7_), channel_id=1, source_target_pairs={{4,8},{8,4},{5,9},{9,5},{6,10},{10,6},{7,11},{11,7},{20,24},{24,20... | collective-permute-start | bytes 786440 | tf_op jit(solution)/shard_map/ppermute | solution.py:531
  22.2 8.3 %collective-permute-start.6 = (bf16[256,512]{1,0:T(8,128)(2,1)S(1)}, bf16[256,512]{1,0:T(8,128)(2,1)S(1)}, u32[]{:S(2)}, u32[]{:S(2)}) collective-permute-start(bf16[256,512]{1,0:T(8,128)(2,1)S(1)} %get-tuple-element.52), channel_id=1, source_target_pairs={{4,8},{8,4},{5,9},{9,5},{6,10},{10,6},{7,11},{11,7},{20,24},{24,20... | collective-permute-start | bytes 786440 | tf_op jit(solution)/shard_map/ppermute | solution.py:535
  22.9 12.9 %collective-permute-start.7 = (bf16[256,512]{1,0:T(8,128)(2,1)S(1)}, bf16[256,512]{1,0:T(8,128)(2,1)S(1)}, u32[]{:S(2)}, u32[]{:S(2)}) collective-permute-start(bf16[256,512]{1,0:T(8,128)(2,1)S(1)} %get-tuple-element.56), channel_id=1, source_target_pairs={{0,4},{4,0},{8,12},{12,8},{1,5},{5,1},{9,13},{13,9},{2,6},{6,2},{1... | collective-permute-start | bytes 786440 | tf_op jit(solution)/shard_map/ppermute | solution.py:534
  28.6 1.0 %copy-start.11 = (bf16[256,512]{1,0:T(8,128)(2,1)S(1)}, bf16[256,512]{1,0:T(8,128)(2,1)}, u32[]{:S(2)}) copy-start(bf16[256,512]{1,0:T(8,128)(2,1)} %get-tuple-element.34.third.third_d) | copy-start | bytes 786436
  28.6 1.0 %copy-start.12 = (bf16[256,512]{1,0:T(8,128)(2,1)S(1)}, bf16[256,512]{1,0:T(8,128)(2,1)}, u32[]{:S(2)}) copy-start(bf16[256,512]{1,0:T(8,128)(2,1)} %get-tuple-element.35.last.last_d) | copy-start | bytes 786436
  29.6 11.3 %collective-permute-start.4 = (bf16[256,512]{1,0:T(8,128)(2,1)S(1)}, bf16[256,512]{1,0:T(8,128)(2,1)S(1)}, u32[]{:S(2)}, u32[]{:S(2)}) collective-permute-start(bf16[256,512]{1,0:T(8,128)(2,1)S(1)} %get-tuple-element.49), channel_id=1, source_target_pairs={{0,4},{4,0},{8,12},{12,8},{1,5},{5,1},{9,13},{13,9},{2,6},{6,2},{1... | collective-permute-start | bytes 786440 | tf_op jit(solution)/shard_map/ppermute | solution.py:541
  29.8 11.2 %collective-permute-start.10 = (bf16[256,512]{1,0:T(8,128)(2,1)S(1)}, bf16[256,512]{1,0:T(8,128)(2,1)S(1)}, u32[]{:S(2)}, u32[]{:S(2)}) collective-permute-start(bf16[256,512]{1,0:T(8,128)(2,1)S(1)} %get-tuple-element.63), channel_id=1, source_target_pairs={{4,8},{8,4},{5,9},{9,5},{6,10},{10,6},{7,11},{11,7},{20,24},{24,20... | collective-permute-start | bytes 786440 | tf_op jit(solution)/shard_map/ppermute | solution.py:539
  36.1 7.8 %collective-permute-start.8 = (bf16[256,512]{1,0:T(8,128)(2,1)S(1)}, bf16[256,512]{1,0:T(8,128)(2,1)S(1)}, u32[]{:S(2)}, u32[]{:S(2)}) collective-permute-start(bf16[256,512]{1,0:T(8,128)(2,1)S(1)} %get-tuple-element.58), channel_id=1, source_target_pairs={{0,4},{12,8},{1,5},{13,9},{2,6},{14,10},{3,7},{15,11},{16,20},{28,... | collective-permute-start | bytes 786440 | tf_op jit(solution)/shard_map/ppermute | solution.py:546
  40.1 4.6 %collective-permute-start.9 = (bf16[256,512]{1,0:T(8,128)(2,1)S(1)}, bf16[256,512]{1,0:T(8,128)(2,1)S(1)}, u32[]{:S(2)}, u32[]{:S(2)}) collective-permute-start(bf16[256,512]{1,0:T(8,128)(2,1)S(1)} %get-tuple-element.61), channel_id=1, source_target_pairs={{4,8},{8,4},{5,9},{9,5},{6,10},{10,6},{7,11},{11,7},{20,24},{24,20... | collective-permute-start | bytes 786440 | tf_op jit(solution)/shard_map/ppermute | solution.py:545
  41.3 8.3 %collective-permute-start.11 = (bf16[256,512]{1,0:T(8,128)(2,1)S(1)}, bf16[256,512]{1,0:T(8,128)(2,1)S(1)}, u32[]{:S(2)}, u32[]{:S(2)}) collective-permute-start(bf16[256,512]{1,0:T(8,128)(2,1)S(1)} %get-tuple-element.64), channel_id=1, source_target_pairs={{4,0},{8,12},{5,1},{9,13},{6,2},{10,14},{7,3},{11,15},{20,16},{24,... | collective-permute-start | bytes 786440 | tf_op jit(solution)/shard_map/ppermute | solution.py:550
  49.8 1.6 %collective-permute-start.12 = (bf16[256,512]{1,0:T(8,128)(2,1)S(1)}, bf16[256,512]{1,0:T(8,128)(2,1)S(1)}, u32[]{:S(2)}, u32[]{:S(2)}) collective-permute-start(bf16[256,512]{1,0:T(8,128)(2,1)S(1)} %term.1), channel_id=1, source_target_pairs={{0,1},{1,0},{2,3},{3,2},{4,5},{5,4},{6,7},{7,6},{8,9},{9,8},{10,11... | collective-permute-start | bytes 786440 | tf_op jit(solution)/shard_map/ppermute | solution.py:574

commit v3 on v2

--- a/solution.py
+++ b/solution.py
@@ -266,8 +266,8 @@
 
 def edge_kernel(held, *refs):
     (
-        routes_in, slots_in, kinds_in, inverse_in, coefs_in, bits_in, images_in, taps_in, col_taps_in, _,
-        weighted, out_edge, _passed,
+        routes_in, slots_in, kinds_in, inverse_in, coefs_in, bits_in, images_in, taps_in, col_taps_in, passed_in,
+        weighted, out_edge, passed,
         routes, slots, kinds, inverse, coefs, bits, images, taps, col_taps, factors, total, sems,
     ) = refs
     strip = lax.axis_index("tile")
@@ -277,7 +277,8 @@
             (coefs_in, coefs), (taps_in, taps), (col_taps_in, col_taps),
         ]
         + in_parts(bits_in, bits, PARTS)
-        + in_parts(images_in, images, PARTS),
+        + in_parts(images_in, images, PARTS)
+        + [(passed_in, passed)],
         sems,
     )
     total[...] = jnp.zeros_like(total)
@@ -301,6 +302,7 @@
             moved, [crosses * coefs[k, kinds[s]] * float(1.0 / scales[k]) for k in range(3)]
         )
     copies[6].wait()
+    copies[-1].wait()
     result = jnp.dot(factors[...], col_taps[...], preferred_element_type=jnp.float32)
     for s in range(held):
         column = 1 + routes[s] * BLOCK_COLS + slots[s] % BLOCK_COLS
@@ -349,7 +351,8 @@
     return pl.ds(pl.multiple_of((1 - lax.axis_index("tile")) * (TILE_ROWS - EDGE), EDGE), EDGE)
 
 
-def relay_kernel(own, got, edge, _after, _, out, _passed):
+def relay_kernel(own, got, edge, *refs):
+    out = refs[-2]
     rows = edge_rows()
     out[...] = code(own[...] + decode(got[...]))
     out[rows] = code(own[rows] + edge[...].astype(jnp.float32) + decode(got[rows]))
@@ -358,6 +361,11 @@
 def plus_kernel(own, got, *refs):
     out = refs[-2]
     out[...] = (own[...].astype(jnp.float32) + got[...].astype(jnp.float32)).astype(jnp.bfloat16)
+
+
+def add_copy_kernel(own, got, share, _after, out, share_out):
+    out[...] = (own[...].astype(jnp.float32) + got[...].astype(jnp.float32)).astype(jnp.bfloat16)
+    share_out[...] = share[...]
 
 
 def at_end():
@@ -465,9 +473,8 @@
     weighted, edge, next_d = pl.pallas_call(
         functools.partial(edge_kernel, held),
         out_shape=[blocks, jax.ShapeDtypeStruct((LINE, EDGE, TILE_COLS), jnp.bfloat16), tile],
-        in_specs=in_hbm(9) + in_place,
-        out_specs=in_vmem(2) + in_place,
-        input_output_aliases={9: 2},
+        in_specs=in_hbm(10),
+        out_specs=in_vmem(3),
         scratch_shapes=[pltpu.SMEM((held,), jnp.int32)]
         + scalars
         + [
@@ -478,7 +485,7 @@
             pltpu.VMEM(col_taps.shape, jnp.bfloat16),
             pltpu.VMEM((held * EDGE, 6 * BLOCK), jnp.bfloat16),
             pltpu.VMEM((columns, EDGE, BLOCK), jnp.float32),
-            pltpu.SemaphoreType.DMA((7 + 2 * PARTS,)),
+            pltpu.SemaphoreType.DMA((8 + 2 * PARTS,)),
         ],
         compiler_params=vmem_limit(24),
         cost_estimate=work(3),
@@ -526,26 +533,35 @@
             name=name,
         )(*operands, *after, passed)
 
+    nothing = jnp.zeros((8, 128), jnp.float32)
     got_far_m = lax.ppermute(far_m, "exp", [(0, 1), (LINE - 1, LINE - 2)])
     far_sum, next_m = passing(plus_kernel, "plus", [far_d, got_far_d], [], next_m)
     mid_far_d = lax.ppermute(far_sum, "exp", across)
     mid_tiles = match(False, [far_sum])
-    next_sum, next_m = passing(plus_kernel, "plus", [next_d, got_next_d], [mid_tiles[0]], next_m)
+    next_sum, next_m = pl.pallas_call(
+        add_copy_kernel,
+        out_shape=[tile, tile],
+        in_specs=in_vmem(3) + in_place,
+        out_specs=in_vmem(2),
+        compiler_params=vmem_limit(24),
+        cost_estimate=work(1),
+        name="plus",
+    )(next_d, got_next_d, next_m, mid_tiles[0])
     got_next_m = lax.ppermute(next_m, "exp", beside)
     mid_d = lax.ppermute(next_sum, "exp", across)
     far_relayed, third_m = passing(
         relay_kernel, "relay", [mid_tiles[0], got_far_m, other_edge[0]], [mid_far_d], third_m
     )
     mid_far_m = lax.ppermute(far_relayed, "exp", across)
-    turned, third_m = passing(turn_kernel, "turn", [third_d, last_d, mid_far_d], [], third_m)
+    turned, _ = passing(turn_kernel, "turn", [third_d, last_d, mid_far_d], [], nothing)
     got_d = lax.ppermute(turned, "exp", beside)
     next_relayed, third_m = passing(
-        relay_kernel, "relay", [mid_tiles[1], got_next_m, other_edge[1]], [mid_d], third_m
+        relay_kernel, "relay", [mid_tiles[1], got_next_m, other_edge[1]], [], third_m
     )
     mid_m = lax.ppermute(next_relayed, "exp", across)
     got_m = lax.ppermute(third_m, "exp", [(0, 1), (LINE - 1, LINE - 2)])
     last_relayed, _ = passing(
-        relay_kernel, "relay", [mid_tiles[3], mid_far_m, other_edge[3]], [got_d], jnp.zeros((8, 128), jnp.float32)
+        relay_kernel, "relay", [mid_tiles[3], mid_far_m, other_edge[3]], [got_d, mid_d], nothing
     )
     end_m = lax.ppermute(last_relayed, "exp", [(1, 0), (LINE - 2, LINE - 1)])
     matched, depth, inverse = pl.pallas_call(

time: 52.7 us -> 51.9 us (0.985)
  waiting for transfers between devices: 12.3 us -> 9.63 us
  starting transfers between devices: 22.9 us -> 25.5 us
  Pallas kernels: 13.8 us -> 12.9 us
    ppermute x1, waiting for transfers between devices: 5.34 us -> 2.14 us  [reduced(): got_next_m = lax.ppermute(next_m, 'exp', beside)]
    ppermute x1, starting transfers between devices: 0.13 us -> 2.98 us  [reduced(): got_d = lax.ppermute(turned, 'exp', beside)]
    ppermute x1, waiting for transfers between devices: 1.36 us -> 2.68 us  [reduced(): got_m = lax.ppermute(third_m, 'exp', [(0, 1), (LINE - 1, LINE - 2)])]
    pallas_call x6 -> x5, Pallas kernels: 2.03 us -> 1.02 us  [passing(): pl.pallas_call(kernel, out_shape=[tile, jax.ShapeDtypeStruct(passed.shape...]
    ppermute x1, waiting for transfers between devices: 4.92 us -> 4.14 us  [reduced(): end_m = lax.ppermute(last_relayed, 'exp', [(1, 0), (LINE - 2, LINE - 1)])]
    unnamed x26 -> x28, local copies, waits for them, and re-layouts: 1.36 us -> 1.62 us
  transfers between devices with their start and end apart: 13 -> 13, of which waited for: 5 -> 5; matrix products, arithmetic and copies ran while one was open for 0% -> 0% of each run, Pallas kernels for 21% -> 20%
where the time goes in v3:
time: 51.9 us; the launch traced here: 51.6 us
  starting transfers between devices  25.5 us (49%)
  Pallas kernels  12.9 us (25%)
  waiting for transfers between devices  9.63 us (19%)
  local copies, waits for them, and re-layouts  1.63 us (3%)
  between operations  1.01 us (2%)
  other arithmetic  0.87 us (2%)
    ppermute x1, starting transfers between devices, reduced(): got_next_m = lax.ppermute(next_m, 'exp', beside)  5.7 us
    ppermute x1, starting transfers between devices, reduced(): got_far_d = lax.ppermute(far_d, 'exp', [(0, 1), (LINE - 1, LINE - 2)])  4.94 us
    pallas_call x2, Pallas kernels, match(): pl.pallas_call(functools.partial(match_kernel, held, ends), out_shape=[wi...  4.47 us
    ppermute x1, waiting for transfers between devices, reduced(): end_m = lax.ppermute(last_relayed, 'exp', [(1, 0), (LINE - 2, LINE - 1)])  4.14 us
    ppermute x1, starting transfers between devices, reduced(): got_m = lax.ppermute(third_m, 'exp', [(0, 1), (LINE - 1, LINE - 2)])  3.66 us
    ppermute x1, starting transfers between devices, reduced(): got_d = lax.ppermute(turned, 'exp', beside)  2.98 us
    ppermute x1, waiting for transfers between devices, reduced(): got_m = lax.ppermute(third_m, 'exp', [(0, 1), (LINE - 1, LINE - 2)])  2.68 us
    pallas_call x1, Pallas kernels, reduced(): pl.pallas_call(functools.partial(edge_kernel, held), out_shape=[blocks, j...  2.66 us
  transfers between devices with their start and end apart: 13, of which 5 were waited for; matrix products, arithmetic and copies ran while one was open for 0% of the time, Pallas kernels for 20%

profile of v3, /device:TPU:0, one launch (start us, length us, event | category | flops | bytes accessed | tf_op | source)
XLA Modules:
  0.0 51.6 jit_solution(10858109891093643339)
XLA Ops:
  0.7 2.5 %depth.1 = (bf16[256,512]{1,0:T(8,128)(2,1)}, bf16[256,512]{1,0:T(8,128)(2,1)}, bf16[256,512]{1,0:T(8,128)(2,1)}, bf16[256,512]{1,0:T(8,128)(2,1)}) custom-call(s32[16]{0:T(128)} %bitcast.17, s32[16]{0:T(128)} %bitcast.21, f32[16]{0:T(128)} %bitcast.31, s32[16,128,128]{2,1,0:T(8,128)} %bitcast.28), custom_call_target="tpu_custom_call" | custom-call | flops 2300000000 | tf_op jit(solution)/shard_map/depth/pallas_call | solution.py:454
  3.2 4.9 %collective-permute-start = (bf16[256,512]{1,0:T(8,128)(2,1)}, bf16[256,512]{1,0:T(8,128)(2,1)S(1)}, u32[]{:S(2)}, u32[]{:S(2)}) collective-permute-start(bf16[256,512]{1,0:T(8,128)(2,1)} %get-tuple-element.35.own), channel_id=1, source_target_pairs={{0,4},{12,8},{1,5},{13,9},{2,6},{14,10},{3,7},{15,11},{16,20},{28,... | collective-permute-start | bytes 786440 | tf_op jit(solution)/shard_map/ppermute | solution.py:469
  8.2 0.6 %copy-done.2 = f32[64,3]{0,1:T(4,128)S(1)} copy-done((f32[64,3]{0,1:T(4,128)S(1)}, f32[64,3]{0,1:T(4,128)}, u32[]{:S(2)}) %copy-start.2) | copy-done | bytes 792
  8.8 0.9 %copy-done.13 = bf16[256,512]{1,0:T(8,128)(2,1)S(1)} copy-done((bf16[256,512]{1,0:T(8,128)(2,1)S(1)}, bf16[256,512]{1,0:T(8,128)(2,1)}, u32[]{:S(2)}) %copy-start.13) | copy-done | bytes 262168
  9.8 2.7 %edges.1 = (bf16[16,128,128]{2,1,0:T(8,128)(2,1)S(1)}, bf16[4,32,512]{2,1,0:T(8,128)(2,1)S(1)}, bf16[256,512]{1,0:T(8,128)(2,1)S(1)}) custom-call(s32[16]{0:T(128)S(1)} %bitcast.18, s32[16]{0:T(128)S(1)} %bitcast.22, s32[16]{0:T(128)S(1)} %bitcast.25, f32[16]{0:T(128)S(1)} %bitcast.32, f32[3,64]{1,0:T(4,128)S(1)} %bitcast.14, s32[16,128,128]{2,1,0:T(8,128)S(1)} %bitcast.29, ...), custom_call_target="tpu_custom_call" | custom-call | flops 3449999872 | tf_op jit(solution)/shard_map/edges/pallas_call | solution.py:473
  12.4 1.6 %collective-permute-start.1 = (bf16[4,32,512]{2,1,0:T(8,128)(2,1)S(1)}, bf16[4,32,512]{2,1,0:T(8,128)(2,1)S(1)}, u32[]{:S(2)}, u32[]{:S(2)}) collective-permute-start(bf16[4,32,512]{2,1,0:T(8,128)(2,1)S(1)} %get-tuple-element.41), channel_id=1, source_target_pairs={{0,2},{2,0},{1,3},{3,1},{4,6},{6,4},{5,7},{7,5},{8,10},{10,8},{9,1... | collective-permute-start | bytes 393224 | tf_op jit(solution)/shard_map/ppermute | solution.py:497
  14.0 1.3 %collective-permute-start.4 = (bf16[256,512]{1,0:T(8,128)(2,1)S(1)}, bf16[256,512]{1,0:T(8,128)(2,1)S(1)}, u32[]{:S(2)}, u32[]{:S(2)}) collective-permute-start(bf16[256,512]{1,0:T(8,128)(2,1)S(1)} %get-tuple-element.45.own), channel_id=1, source_target_pairs={{0,4},{12,8},{1,5},{13,9},{2,6},{14,10},{3,7},{15,11},{16,20},{28,... | collective-permute-start | bytes 786440 | tf_op jit(solution)/shard_map/ppermute | solution.py:498
  15.3 3.9 %match.2 = (f32[256,512]{1,0:T(8,128)S(1)}, f32[256,512]{1,0:T(8,128)S(1)}, f32[256,512]{1,0:T(8,128)S(1)}, f32[256,512]{1,0:T(8,128)S(1)}) custom-call(s32[16]{0:T(128)S(1)} %bitcast.19, s32[16]{0:T(128)S(1)} %bitcast.23, s32[16]{0:T(128)S(1)} %bitcast.26, f32[3,64]{1,0:T(4,128)S(1)} %bitcast.15, bf16[16,128,128]{2,1,0:T(8,128)(2,1)S(1)} %get-tuple-element.37.refs_4_, ...), custom_call_target="tpu_custom_call" | custom-call | tf_op jit(solution)/shard_map/match/pallas_call | solution.py:502
  19.2 0.2 first.1
  19.4 1.3 %collective-permute-start.7 = (bf16[256,512]{1,0:T(8,128)(2,1)S(1)}, bf16[256,512]{1,0:T(8,128)(2,1)S(1)}, u32[]{:S(2)}, u32[]{:S(2)}) collective-permute-start(bf16[256,512]{1,0:T(8,128)(2,1)S(1)} %get-tuple-element.53), channel_id=1, source_target_pairs={{0,4},{12,8},{1,5},{13,9},{2,6},{14,10},{3,7},{15,11},{16,20},{28,... | collective-permute-start | bytes 786440 | tf_op jit(solution)/shard_map/ppermute | solution.py:537
  20.8 0.7 %collective-permute-start.2 = (bf16[256,512]{1,0:T(8,128)(2,1)S(1)}, bf16[256,512]{1,0:T(8,128)(2,1)S(1)}, u32[]{:S(2)}, u32[]{:S(2)}) collective-permute-start(bf16[256,512]{1,0:T(8,128)(2,1)S(1)} %get-tuple-element.43.refs_7_), channel_id=1, source_target_pairs={{4,8},{8,4},{5,9},{9,5},{6,10},{10,6},{7,11},{11,7},{20,24},{24,20... | collective-permute-start | bytes 786440 | tf_op jit(solution)/shard_map/ppermute | solution.py:539
  21.5 0.6 %match.3 = (f32[256,512]{1,0:T(8,128)S(1)}, f32[256,512]{1,0:T(8,128)S(1)}, f32[256,512]{1,0:T(8,128)S(1)}, f32[256,512]{1,0:T(8,128)S(1)}) custom-call(s32[16]{0:T(128)S(1)} %bitcast.20, s32[16]{0:T(128)S(1)} %bitcast.24, s32[16]{0:T(128)S(1)} %bitcast.27, f32[3,64]{1,0:T(4,128)S(1)} %bitcast.16, bf16[16,128,128]{2,1,0:T(8,128)(2,1)S(1)} %get-tuple-element.37.refs_4_, ...), custom_call_target="tpu_custom_call" | custom-call | tf_op jit(solution)/shard_map/match/pallas_call | solution.py:502
  22.1 0.1 plus.3
  22.2 0.7 %collective-permute-start.5 = (bf16[256,512]{1,0:T(8,128)(2,1)S(1)}, bf16[256,512]{1,0:T(8,128)(2,1)S(1)}, u32[]{:S(2)}, u32[]{:S(2)}) collective-permute-start(bf16[256,512]{1,0:T(8,128)(2,1)S(1)} %get-tuple-element.48), channel_id=1, source_target_pairs={{4,8},{8,4},{5,9},{9,5},{6,10},{10,6},{7,11},{11,7},{20,24},{24,20... | collective-permute-start | bytes 786440 | tf_op jit(solution)/shard_map/ppermute | solution.py:551
  22.9 5.7 %collective-permute-start.6 = (bf16[256,512]{1,0:T(8,128)(2,1)S(1)}, bf16[256,512]{1,0:T(8,128)(2,1)S(1)}, u32[]{:S(2)}, u32[]{:S(2)}) collective-permute-start(bf16[256,512]{1,0:T(8,128)(2,1)S(1)} %get-tuple-element.52), channel_id=1, source_target_pairs={{0,4},{4,0},{8,12},{12,8},{1,5},{5,1},{9,13},{13,9},{2,6},{6,2},{1... | collective-permute-start | bytes 786440 | tf_op jit(solution)/shard_map/ppermute | solution.py:550
  28.6 0.3 relay.3
  28.9 0.7 %collective-permute-start.10 = (bf16[256,512]{1,0:T(8,128)(2,1)S(1)}, bf16[256,512]{1,0:T(8,128)(2,1)S(1)}, u32[]{:S(2)}, u32[]{:S(2)}) collective-permute-start(bf16[256,512]{1,0:T(8,128)(2,1)S(1)} %get-tuple-element.61), channel_id=1, source_target_pairs={{4,8},{8,4},{5,9},{9,5},{6,10},{10,6},{7,11},{11,7},{20,24},{24,20... | collective-permute-start | bytes 786440 | tf_op jit(solution)/shard_map/ppermute | solution.py:555
  29.7 3.0 %collective-permute-start.3 = (bf16[256,512]{1,0:T(8,128)(2,1)S(1)}, bf16[256,512]{1,0:T(8,128)(2,1)S(1)}, u32[]{:S(2)}, u32[]{:S(2)}) collective-permute-start(bf16[256,512]{1,0:T(8,128)(2,1)S(1)} %get-tuple-element.44), channel_id=1, source_target_pairs={{0,4},{4,0},{8,12},{12,8},{1,5},{5,1},{9,13},{13,9},{2,6},{6,2},{1... | collective-permute-start | bytes 786440 | tf_op jit(solution)/shard_map/ppermute | solution.py:557
  32.6 2.1 %collective-permute-done.6.got = bf16[256,512]{1,0:T(8,128)(2,1)S(1)} collective-permute-done((bf16[256,512]{1,0:T(8,128)(2,1)S(1)}, bf16[256,512]{1,0:T(8,128)(2,1)S(1)}, u32[]{:S(2)}, u32[]{:S(2)}) %collective-permute-start.6) | collective-permute-done | bytes 262176 | tf_op jit(solution)/shard_map/ppermute | solution.py:550
  34.8 0.3 relay.4
  35.1 3.7 %collective-permute-start.8 = (bf16[256,512]{1,0:T(8,128)(2,1)S(1)}, bf16[256,512]{1,0:T(8,128)(2,1)S(1)}, u32[]{:S(2)}, u32[]{:S(2)}) collective-permute-start(bf16[256,512]{1,0:T(8,128)(2,1)S(1)} %get-tuple-element.56), channel_id=1, source_target_pairs={{0,4},{12,8},{1,5},{13,9},{2,6},{14,10},{3,7},{15,11},{16,20},{28,... | collective-permute-start | bytes 786440 | tf_op jit(solution)/shard_map/ppermute | solution.py:562
  38.8 0.7 %collective-permute-start.9 = (bf16[256,512]{1,0:T(8,128)(2,1)S(1)}, bf16[256,512]{1,0:T(8,128)(2,1)S(1)}, u32[]{:S(2)}, u32[]{:S(2)}) collective-permute-start(bf16[256,512]{1,0:T(8,128)(2,1)S(1)} %get-tuple-element.59), channel_id=1, source_target_pairs={{4,8},{8,4},{5,9},{9,5},{6,10},{10,6},{7,11},{11,7},{20,24},{24,20... | collective-permute-start | bytes 786440 | tf_op jit(solution)/shard_map/ppermute | solution.py:561
  39.5 0.2 collective-permute-done.3.got_d.refs_0_
  39.7 0.3 relay.5
  40.0 1.3 %collective-permute-start.11 = (bf16[256,512]{1,0:T(8,128)(2,1)S(1)}, bf16[256,512]{1,0:T(8,128)(2,1)S(1)}, u32[]{:S(2)}, u32[]{:S(2)}) collective-permute-start(bf16[256,512]{1,0:T(8,128)(2,1)S(1)} %get-tuple-element.62), channel_id=1, source_target_pairs={{4,0},{8,12},{5,1},{9,13},{6,2},{10,14},{7,3},{11,15},{20,16},{24,... | collective-permute-start | bytes 786440 | tf_op jit(solution)/shard_map/ppermute | solution.py:566
  41.3 2.7 %collective-permute-done.8.got_m = bf16[256,512]{1,0:T(8,128)(2,1)S(1)} collective-permute-done((bf16[256,512]{1,0:T(8,128)(2,1)S(1)}, bf16[256,512]{1,0:T(8,128)(2,1)S(1)}, u32[]{:S(2)}, u32[]{:S(2)}) %collective-permute-start.8) | collective-permute-done | bytes 262176 | tf_op jit(solution)/shard_map/ppermute | solution.py:562
  44.0 0.7 %gather.1 = (f32[256,512]{1,0:T(8,128)S(1)}, f32[256,512]{1,0:T(8,128)S(1)}, f32[256,512]{1,0:T(8,128)S(1)}) custom-call(bf16[256,512]{1,0:T(8,128)(2,1)S(1)} %copy-done.11, bf16[256,512]{1,0:T(8,128)(2,1)S(1)} %copy-done.12, bf16[256,512]{1,0:T(8,128)(2,1)S(1)} %collective-permute-done.3.got_d.refs_0_, ...), custom_call_target="tpu_custom_call" | custom-call | flops 1150000000 | tf_op jit(solution)/shard_map/gather/pallas_call | solution.py:567
  44.7 4.1 %collective-permute-done.11.got_last_m = bf16[256,512]{1,0:T(8,128)(2,1)S(1)} collective-permute-done((bf16[256,512]{1,0:T(8,128)(2,1)S(1)}, bf16[256,512]{1,0:T(8,128)(2,1)S(1)}, u32[]{:S(2)}, u32[]{:S(2)}) %collective-permute-start.11) | collective-permute-done | bytes 262176 | tf_op jit(solution)/shard_map/ppermute | solution.py:566
  48.8 0.3 term.1
  49.2 1.1 %coadd.1 = f32[256,512]{1,0:T(8,128)} custom-call(f32[256,512]{1,0:T(8,128)S(1)} %get-tuple-element.57.matched, f32[256,512]{1,0:T(8,128)S(1)} %get-tuple-element.58.inverse, bf16[256,512]{1,0:T(8,128)(2,1)S(1)} %collective-permute-done.9.got_mid_m, bf16[256,512]{1,0:T(8,128)(2,1)S(1)} %collective-permute-done.11.got_last_m), custom_call_target="tpu_custom_call" | custom-call | flops 1150000000 | tf_op jit(solution)/shard_map/coadd/pallas_call | solution.py:578
  50.3 0.5 collective-permute-done.12
  50.7 0.9 %convert_add_fusion = f32[256,512]{1,0:T(8,128)} fusion(bf16[256,512]{1,0:T(8,128)(2,1)S(1)} %collective-permute-done.12, bf16[256,512]{1,0:T(8,128)(2,1)S(1)} %term.1), kind=kLoop, calls=%fused_computation | loop fusion | flops 393216 | bytes 1048576 | tf_op jit(solution)/shard_map/add | solution.py:591
  (40 shorter events, 0.3 us)
Async XLA Ops:
  0.6 7.5 %copy-start = (bf16[768,256]{1,0:T(8,128)(2,1)S(1)}, bf16[768,256]{1,0:T(8,128)(2,1)}, u32[]{:S(2)}) copy-start(bf16[768,256]{1,0:T(8,128)(2,1)} %constant.8.clone.refs_8_.refs_6_) | copy-start | bytes 1179652
  0.6 7.5 %copy-start.6 = (s32[1,1,16,128,128]{4,3,2,1,0:T(8,128)S(1)}, s32[1,1,16,128,128]{4,3,2,1,0:T(8,128)}, u32[]{:S(2)}) copy-start(s32[1,1,16,128,128]{4,3,2,1,0:T(8,128)} %param.11) | copy-start | bytes 3145732
  0.7 7.5 %copy-start.7 = (bf16[1,1,16,128,128]{4,3,2,1,0:T(8,128)(2,1)S(1)}, bf16[1,1,16,128,128]{4,3,2,1,0:T(8,128)(2,1)}, u32[]{:S(2)}) copy-start(bf16[1,1,16,128,128]{4,3,2,1,0:T(8,128)(2,1)} %param.10) | copy-start | bytes 1572868
  0.7 7.5 %copy-start.9 = (f32[1,1,16]{2,1,0:T(1,128)S(1)}, f32[1,1,16]{2,1,0:T(1,128)}, u32[]{:S(2)}) copy-start(f32[1,1,16]{2,1,0:T(1,128)} %param.12) | copy-start | bytes 196
  0.7 7.5 %copy-start.10 = (bf16[2,96,256]{2,1,0:T(8,128)(2,1)S(1)}, bf16[2,96,256]{2,1,0:T(8,128)(2,1)}, u32[]{:S(2)}) copy-start(bf16[2,96,256]{2,1,0:T(8,128)(2,1)} %constant.9.clone.refs_7_) | copy-start | bytes 294916
  3.2 17.5 %collective-permute-start = (bf16[256,512]{1,0:T(8,128)(2,1)}, bf16[256,512]{1,0:T(8,128)(2,1)S(1)}, u32[]{:S(2)}, u32[]{:S(2)}) collective-permute-start(bf16[256,512]{1,0:T(8,128)(2,1)} %get-tuple-element.35.own), channel_id=1, source_target_pairs={{0,4},{12,8},{1,5},{13,9},{2,6},{14,10},{3,7},{15,11},{16,20},{28,... | collective-permute-start | bytes 786440 | tf_op jit(solution)/shard_map/ppermute | solution.py:469
  8.1 0.7 %copy-start.2 = (f32[64,3]{0,1:T(4,128)S(1)}, f32[64,3]{0,1:T(4,128)}, u32[]{:S(2)}) copy-start(f32[64,3]{0,1:T(4,128)} %param.16) | copy-start | bytes 2308
  8.1 0.7 %copy-start.3 = (s32[1,1,16,1]{2,3,1,0:T(1,128)S(1)}, s32[1,1,16,1]{2,3,1,0:T(1,128)}, u32[]{:S(2)}) copy-start(s32[1,1,16,1]{2,3,1,0:T(1,128)} %param.13) | copy-start | bytes 196
  8.1 0.7 %copy-start.4 = (s32[1,1,16]{2,1,0:T(1,128)S(1)}, s32[1,1,16]{2,1,0:T(1,128)}, u32[]{:S(2)}) copy-start(s32[1,1,16]{2,1,0:T(1,128)} %param.14) | copy-start | bytes 196
  8.1 0.7 %copy-start.5 = (s32[1,1,16]{2,1,0:T(1,128)S(1)}, s32[1,1,16]{2,1,0:T(1,128)}, u32[]{:S(2)}) copy-start(s32[1,1,16]{2,1,0:T(1,128)} %param.15) | copy-start | bytes 196
  8.8 0.9 %copy-start.13 = (bf16[256,512]{1,0:T(8,128)(2,1)S(1)}, bf16[256,512]{1,0:T(8,128)(2,1)}, u32[]{:S(2)}) copy-start(bf16[256,512]{1,0:T(8,128)(2,1)} %get-tuple-element.36.refs_9_) | copy-start | bytes 786436
  9.8 5.5 %copy-start.1 = (bf16[528,256]{1,0:T(8,128)(2,1)S(1)}, bf16[528,256]{1,0:T(8,128)(2,1)}, u32[]{:S(2)}) copy-start(bf16[528,256]{1,0:T(8,128)(2,1)} %constant.10.clone.refs_5_) | copy-start | bytes 811012
  12.4 6.8 %collective-permute-start.1 = (bf16[4,32,512]{2,1,0:T(8,128)(2,1)S(1)}, bf16[4,32,512]{2,1,0:T(8,128)(2,1)S(1)}, u32[]{:S(2)}, u32[]{:S(2)}) collective-permute-start(bf16[4,32,512]{2,1,0:T(8,128)(2,1)S(1)} %get-tuple-element.41), channel_id=1, source_target_pairs={{0,2},{2,0},{1,3},{3,1},{4,6},{6,4},{5,7},{7,5},{8,10},{10,8},{9,1... | collective-permute-start | bytes 393224 | tf_op jit(solution)/shard_map/ppermute | solution.py:497
  14.0 8.1 %collective-permute-start.4 = (bf16[256,512]{1,0:T(8,128)(2,1)S(1)}, bf16[256,512]{1,0:T(8,128)(2,1)S(1)}, u32[]{:S(2)}, u32[]{:S(2)}) collective-permute-start(bf16[256,512]{1,0:T(8,128)(2,1)S(1)} %get-tuple-element.45.own), channel_id=1, source_target_pairs={{0,4},{12,8},{1,5},{13,9},{2,6},{14,10},{3,7},{15,11},{16,20},{28,... | collective-permute-start | bytes 786440 | tf_op jit(solution)/shard_map/ppermute | solution.py:498
  19.2 1.5 %copy-start.8 = (bf16[256,512]{1,0:T(8,128)(2,1)S(1)}, bf16[256,512]{1,0:T(8,128)(2,1)}, u32[]{:S(2)}) copy-start(bf16[256,512]{1,0:T(8,128)(2,1)} %get-tuple-element.35.own) | copy-start | bytes 786436
  19.4 9.2 %collective-permute-start.7 = (bf16[256,512]{1,0:T(8,128)(2,1)S(1)}, bf16[256,512]{1,0:T(8,128)(2,1)S(1)}, u32[]{:S(2)}, u32[]{:S(2)}) collective-permute-start(bf16[256,512]{1,0:T(8,128)(2,1)S(1)} %get-tuple-element.53), channel_id=1, source_target_pairs={{0,4},{12,8},{1,5},{13,9},{2,6},{14,10},{3,7},{15,11},{16,20},{28,... | collective-permute-start | bytes 786440 | tf_op jit(solution)/shard_map/ppermute | solution.py:537
  20.8 7.8 %collective-permute-start.2 = (bf16[256,512]{1,0:T(8,128)(2,1)S(1)}, bf16[256,512]{1,0:T(8,128)(2,1)S(1)}, u32[]{:S(2)}, u32[]{:S(2)}) collective-permute-start(bf16[256,512]{1,0:T(8,128)(2,1)S(1)} %get-tuple-element.43.refs_7_), channel_id=1, source_target_pairs={{4,8},{8,4},{5,9},{9,5},{6,10},{10,6},{7,11},{11,7},{20,24},{24,20... | collective-permute-start | bytes 786440 | tf_op jit(solution)/shard_map/ppermute | solution.py:539
  22.2 17.3 %collective-permute-start.5 = (bf16[256,512]{1,0:T(8,128)(2,1)S(1)}, bf16[256,512]{1,0:T(8,128)(2,1)S(1)}, u32[]{:S(2)}, u32[]{:S(2)}) collective-permute-start(bf16[256,512]{1,0:T(8,128)(2,1)S(1)} %get-tuple-element.48), channel_id=1, source_target_pairs={{4,8},{8,4},{5,9},{9,5},{6,10},{10,6},{7,11},{11,7},{20,24},{24,20... | collective-permute-start | bytes 786440 | tf_op jit(solution)/shard_map/ppermute | solution.py:551
  22.9 11.9 %collective-permute-start.6 = (bf16[256,512]{1,0:T(8,128)(2,1)S(1)}, bf16[256,512]{1,0:T(8,128)(2,1)S(1)}, u32[]{:S(2)}, u32[]{:S(2)}) collective-permute-start(bf16[256,512]{1,0:T(8,128)(2,1)S(1)} %get-tuple-element.52), channel_id=1, source_target_pairs={{0,4},{4,0},{8,12},{12,8},{1,5},{5,1},{9,13},{13,9},{2,6},{6,2},{1... | collective-permute-start | bytes 786440 | tf_op jit(solution)/shard_map/ppermute | solution.py:550
  28.6 1.0 %copy-start.11 = (bf16[256,512]{1,0:T(8,128)(2,1)S(1)}, bf16[256,512]{1,0:T(8,128)(2,1)}, u32[]{:S(2)}) copy-start(bf16[256,512]{1,0:T(8,128)(2,1)} %get-tuple-element.33.third.third_d) | copy-start | bytes 786436
  28.6 1.0 %copy-start.12 = (bf16[256,512]{1,0:T(8,128)(2,1)S(1)}, bf16[256,512]{1,0:T(8,128)(2,1)}, u32[]{:S(2)}) copy-start(bf16[256,512]{1,0:T(8,128)(2,1)} %get-tuple-element.34.last.last_d) | copy-start | bytes 786436
  28.9 10.6 %collective-permute-start.10 = (bf16[256,512]{1,0:T(8,128)(2,1)S(1)}, bf16[256,512]{1,0:T(8,128)(2,1)S(1)}, u32[]{:S(2)}, u32[]{:S(2)}) collective-permute-start(bf16[256,512]{1,0:T(8,128)(2,1)S(1)} %get-tuple-element.61), channel_id=1, source_target_pairs={{4,8},{8,4},{5,9},{9,5},{6,10},{10,6},{7,11},{11,7},{20,24},{24,20... | collective-permute-start | bytes 786440 | tf_op jit(solution)/shard_map/ppermute | solution.py:555
  29.7 10.0 %collective-permute-start.3 = (bf16[256,512]{1,0:T(8,128)(2,1)S(1)}, bf16[256,512]{1,0:T(8,128)(2,1)S(1)}, u32[]{:S(2)}, u32[]{:S(2)}) collective-permute-start(bf16[256,512]{1,0:T(8,128)(2,1)S(1)} %get-tuple-element.44), channel_id=1, source_target_pairs={{0,4},{4,0},{8,12},{12,8},{1,5},{5,1},{9,13},{13,9},{2,6},{6,2},{1... | collective-permute-start | bytes 786440 | tf_op jit(solution)/shard_map/ppermute | solution.py:557
  35.1 8.9 %collective-permute-start.8 = (bf16[256,512]{1,0:T(8,128)(2,1)S(1)}, bf16[256,512]{1,0:T(8,128)(2,1)S(1)}, u32[]{:S(2)}, u32[]{:S(2)}) collective-permute-start(bf16[256,512]{1,0:T(8,128)(2,1)S(1)} %get-tuple-element.56), channel_id=1, source_target_pairs={{0,4},{12,8},{1,5},{13,9},{2,6},{14,10},{3,7},{15,11},{16,20},{28,... | collective-permute-start | bytes 786440 | tf_op jit(solution)/shard_map/ppermute | solution.py:562
  38.8 5.9 %collective-permute-start.9 = (bf16[256,512]{1,0:T(8,128)(2,1)S(1)}, bf16[256,512]{1,0:T(8,128)(2,1)S(1)}, u32[]{:S(2)}, u32[]{:S(2)}) collective-permute-start(bf16[256,512]{1,0:T(8,128)(2,1)S(1)} %get-tuple-element.59), channel_id=1, source_target_pairs={{4,8},{8,4},{5,9},{9,5},{6,10},{10,6},{7,11},{11,7},{20,24},{24,20... | collective-permute-start | bytes 786440 | tf_op jit(solution)/shard_map/ppermute | solution.py:561
  40.0 8.8 %collective-permute-start.11 = (bf16[256,512]{1,0:T(8,128)(2,1)S(1)}, bf16[256,512]{1,0:T(8,128)(2,1)S(1)}, u32[]{:S(2)}, u32[]{:S(2)}) collective-permute-start(bf16[256,512]{1,0:T(8,128)(2,1)S(1)} %get-tuple-element.62), channel_id=1, source_target_pairs={{4,0},{8,12},{5,1},{9,13},{6,2},{10,14},{7,3},{11,15},{20,16},{24,... | collective-permute-start | bytes 786440 | tf_op jit(solution)/shard_map/ppermute | solution.py:566
  49.1 1.6 %collective-permute-start.12 = (bf16[256,512]{1,0:T(8,128)(2,1)S(1)}, bf16[256,512]{1,0:T(8,128)(2,1)S(1)}, u32[]{:S(2)}, u32[]{:S(2)}) collective-permute-start(bf16[256,512]{1,0:T(8,128)(2,1)S(1)} %term.1), channel_id=1, source_target_pairs={{0,1},{1,0},{2,3},{3,2},{4,5},{5,4},{6,7},{7,6},{8,9},{9,8},{10,11... | collective-permute-start | bytes 786440 | tf_op jit(solution)/shard_map/ppermute | solution.py:590

commit v4 on v3

--- a/solution.py
+++ b/solution.py
@@ -324,22 +324,25 @@
     total = refs[-1]
     total[...] = jnp.zeros_like(total)
     scales = tap_scales()
-    for first in range(0, held, 2):
-        both = jnp.concatenate([weighted[first], weighted[first + 1]], axis=1)
-        moved = jnp.dot(
-            taps[...], jnp.concatenate([both, both], axis=0), preferred_element_type=jnp.float32
+    size = BLOCK + 2 * REACH
+    for start in range(0, held, 4):
+        factors = []
+        for first in range(start, start + 4, 2):
+            both = jnp.concatenate([weighted[first], weighted[first + 1]], axis=1)
+            moved = jnp.dot(
+                taps[...], jnp.concatenate([both, both], axis=0), preferred_element_type=jnp.float32
+            )
+            for n in range(2):
+                mixing = [coefs[k, kinds[first + n]] * float(1.0 / scales[k]) for k in range(3)]
+                factors.append(split_rows(moved[:, n * BLOCK : (n + 1) * BLOCK], mixing))
+        result = jnp.dot(
+            jnp.concatenate(factors, axis=0), col_taps[...], preferred_element_type=jnp.float32
         )
-        for n in range(2):
-            s = first + n
-            slot = slots[s]
-            factors = split_rows(
-                moved[:, n * BLOCK : (n + 1) * BLOCK],
-                [coefs[k, kinds[s]] * float(1.0 / scales[k]) for k in range(3)],
-            )
-            result = jnp.dot(factors, col_taps[...], preferred_element_type=jnp.float32)
+        for n in range(4):
+            slot = slots[start + n]
             row = pl.multiple_of(slot // BLOCK_COLS * BLOCK, 8)
-            column = 1 + routes[s] * BLOCK_COLS + slot % BLOCK_COLS
-            spread_columns(total, column, pl.ds(row, BLOCK + 2 * REACH), result)
+            column = 1 + routes[start + n] * BLOCK_COLS + slot % BLOCK_COLS
+            spread_columns(total, column, pl.ds(row, size), result[n * size : (n + 1) * size])
     for place in range(LINE):
         for b in range(BLOCK_COLS):
             out_tiles[place][:, b * BLOCK : (b + 1) * BLOCK] = total[

time: 51.9 us -> 51.1 us (0.985)
  waiting for transfers between devices: 9.63 us -> 8.84 us
  Pallas kernels: 12.9 us -> 12.2 us
  starting transfers between devices: 25.5 us -> 26.2 us
    ppermute x1, waiting for transfers between devices: 2.14 us -> 0.29 us  [reduced(): got_next_m = lax.ppermute(next_m, 'exp', beside)]
    ppermute x1, waiting for transfers between devices: 0.19 us -> 1.79 us  [reduced(): got_d = lax.ppermute(turned, 'exp', beside)]
    pallas_call x2, Pallas kernels: 4.47 us -> 3.78 us  [match(): pl.pallas_call(functools.partial(match_kernel, held, ends), out_shape=[wi...]
    ppermute x1, starting transfers between devices: 2.98 us -> 3.66 us  [reduced(): got_d = lax.ppermute(turned, 'exp', beside)]
  transfers between devices with their start and end apart: 13 -> 13, of which waited for: 5 -> 5; matrix products, arithmetic and copies ran while one was open for 0% -> 0% of each run, Pallas kernels for 20% -> 19%
where the time goes in v4:
time: 51.1 us; the launch traced here: 50.8 us
  starting transfers between devices  26.2 us (51%)
  Pallas kernels  12.2 us (24%)
  waiting for transfers between devices  8.84 us (17%)
  local copies, waits for them, and re-layouts  1.63 us (3%)
  between operations  1.01 us (2%)
  other arithmetic  0.87 us (2%)
    ppermute x1, starting transfers between devices, reduced(): got_next_m = lax.ppermute(next_m, 'exp', beside)  5.71 us
    ppermute x1, starting transfers between devices, reduced(): got_far_d = lax.ppermute(far_d, 'exp', [(0, 1), (LINE - 1, LINE - 2)])  4.94 us
    ppermute x1, waiting for transfers between devices, reduced(): end_m = lax.ppermute(last_relayed, 'exp', [(1, 0), (LINE - 2, LINE - 1)])  4.06 us
    pallas_call x2, Pallas kernels, match(): pl.pallas_call(functools.partial(match_kernel, held, ends), out_shape=[wi...  3.78 us
    ppermute x1, starting transfers between devices, reduced(): got_d = lax.ppermute(turned, 'exp', beside)  3.66 us
    ppermute x1, starting transfers between devices, reduced(): got_m = lax.ppermute(third_m, 'exp', [(0, 1), (LINE - 1, LINE - 2)])  3.66 us
    pallas_call x1, Pallas kernels, reduced(): pl.pallas_call(functools.partial(edge_kernel, held), out_shape=[blocks, j...  2.66 us
    pallas_call x1, Pallas kernels, reduced(): pl.pallas_call(functools.partial(depth_kernel, held), out_shape=[tile] *...  2.47 us
  transfers between devices with their start and end apart: 13, of which 5 were waited for; matrix products, arithmetic and copies ran while one was open for 0% of the time, Pallas kernels for 19%

profile of v4, /device:TPU:0, one launch (start us, length us, event | category | flops | bytes accessed | tf_op | source)
XLA Modules:
  0.0 50.8 jit_solution(6283561180793472909)
XLA Ops:
  0.7 2.5 %depth.1 = (bf16[256,512]{1,0:T(8,128)(2,1)}, bf16[256,512]{1,0:T(8,128)(2,1)}, bf16[256,512]{1,0:T(8,128)(2,1)}, bf16[256,512]{1,0:T(8,128)(2,1)}) custom-call(s32[16]{0:T(128)} %bitcast.17, s32[16]{0:T(128)} %bitcast.21, f32[16]{0:T(128)} %bitcast.31, s32[16,128,128]{2,1,0:T(8,128)} %bitcast.28), custom_call_target="tpu_custom_call" | custom-call | flops 2300000000 | tf_op jit(solution)/shard_map/depth/pallas_call | solution.py:457
  3.2 4.9 %collective-permute-start = (bf16[256,512]{1,0:T(8,128)(2,1)}, bf16[256,512]{1,0:T(8,128)(2,1)S(1)}, u32[]{:S(2)}, u32[]{:S(2)}) collective-permute-start(bf16[256,512]{1,0:T(8,128)(2,1)} %get-tuple-element.35.own), channel_id=1, source_target_pairs={{0,4},{12,8},{1,5},{13,9},{2,6},{14,10},{3,7},{15,11},{16,20},{28,... | collective-permute-start | bytes 786440 | tf_op jit(solution)/shard_map/ppermute | solution.py:472
  8.2 0.6 %copy-done.2 = f32[64,3]{0,1:T(4,128)S(1)} copy-done((f32[64,3]{0,1:T(4,128)S(1)}, f32[64,3]{0,1:T(4,128)}, u32[]{:S(2)}) %copy-start.2) | copy-done | bytes 792
  8.8 0.9 %copy-done.13 = bf16[256,512]{1,0:T(8,128)(2,1)S(1)} copy-done((bf16[256,512]{1,0:T(8,128)(2,1)S(1)}, bf16[256,512]{1,0:T(8,128)(2,1)}, u32[]{:S(2)}) %copy-start.13) | copy-done | bytes 262168
  9.8 2.7 %edges.1 = (bf16[16,128,128]{2,1,0:T(8,128)(2,1)S(1)}, bf16[4,32,512]{2,1,0:T(8,128)(2,1)S(1)}, bf16[256,512]{1,0:T(8,128)(2,1)S(1)}) custom-call(s32[16]{0:T(128)S(1)} %bitcast.18, s32[16]{0:T(128)S(1)} %bitcast.22, s32[16]{0:T(128)S(1)} %bitcast.25, f32[16]{0:T(128)S(1)} %bitcast.32, f32[3,64]{1,0:T(4,128)S(1)} %bitcast.14, s32[16,128,128]{2,1,0:T(8,128)S(1)} %bitcast.29, ...), custom_call_target="tpu_custom_call" | custom-call | flops 3449999872 | tf_op jit(solution)/shard_map/edges/pallas_call | solution.py:476
  12.4 1.6 %collective-permute-start.1 = (bf16[4,32,512]{2,1,0:T(8,128)(2,1)S(1)}, bf16[4,32,512]{2,1,0:T(8,128)(2,1)S(1)}, u32[]{:S(2)}, u32[]{:S(2)}) collective-permute-start(bf16[4,32,512]{2,1,0:T(8,128)(2,1)S(1)} %get-tuple-element.41), channel_id=1, source_target_pairs={{0,2},{2,0},{1,3},{3,1},{4,6},{6,4},{5,7},{7,5},{8,10},{10,8},{9,1... | collective-permute-start | bytes 393224 | tf_op jit(solution)/shard_map/ppermute | solution.py:500
  14.0 1.3 %collective-permute-start.4 = (bf16[256,512]{1,0:T(8,128)(2,1)S(1)}, bf16[256,512]{1,0:T(8,128)(2,1)S(1)}, u32[]{:S(2)}, u32[]{:S(2)}) collective-permute-start(bf16[256,512]{1,0:T(8,128)(2,1)S(1)} %get-tuple-element.45.own), channel_id=1, source_target_pairs={{0,4},{12,8},{1,5},{13,9},{2,6},{14,10},{3,7},{15,11},{16,20},{28,... | collective-permute-start | bytes 786440 | tf_op jit(solution)/shard_map/ppermute | solution.py:501
  15.3 3.2 %match.2 = (f32[256,512]{1,0:T(8,128)S(1)}, f32[256,512]{1,0:T(8,128)S(1)}, f32[256,512]{1,0:T(8,128)S(1)}, f32[256,512]{1,0:T(8,128)S(1)}) custom-call(s32[16]{0:T(128)S(1)} %bitcast.19, s32[16]{0:T(128)S(1)} %bitcast.23, s32[16]{0:T(128)S(1)} %bitcast.26, f32[3,64]{1,0:T(4,128)S(1)} %bitcast.15, bf16[16,128,128]{2,1,0:T(8,128)(2,1)S(1)} %get-tuple-element.37.refs_4_, ...), custom_call_target="tpu_custom_call" | custom-call | tf_op jit(solution)/shard_map/match/pallas_call | solution.py:505
  18.5 0.2 first.1
  18.7 1.3 %collective-permute-start.7 = (bf16[256,512]{1,0:T(8,128)(2,1)S(1)}, bf16[256,512]{1,0:T(8,128)(2,1)S(1)}, u32[]{:S(2)}, u32[]{:S(2)}) collective-permute-start(bf16[256,512]{1,0:T(8,128)(2,1)S(1)} %get-tuple-element.53), channel_id=1, source_target_pairs={{0,4},{12,8},{1,5},{13,9},{2,6},{14,10},{3,7},{15,11},{16,20},{28,... | collective-permute-start | bytes 786440 | tf_op jit(solution)/shard_map/ppermute | solution.py:540
  20.1 0.7 %collective-permute-start.2 = (bf16[256,512]{1,0:T(8,128)(2,1)S(1)}, bf16[256,512]{1,0:T(8,128)(2,1)S(1)}, u32[]{:S(2)}, u32[]{:S(2)}) collective-permute-start(bf16[256,512]{1,0:T(8,128)(2,1)S(1)} %get-tuple-element.43.refs_7_), channel_id=1, source_target_pairs={{4,8},{8,4},{5,9},{9,5},{6,10},{10,6},{7,11},{11,7},{20,24},{24,20... | collective-permute-start | bytes 786440 | tf_op jit(solution)/shard_map/ppermute | solution.py:542
  20.8 0.6 %match.3 = (f32[256,512]{1,0:T(8,128)S(1)}, f32[256,512]{1,0:T(8,128)S(1)}, f32[256,512]{1,0:T(8,128)S(1)}, f32[256,512]{1,0:T(8,128)S(1)}) custom-call(s32[16]{0:T(128)S(1)} %bitcast.20, s32[16]{0:T(128)S(1)} %bitcast.24, s32[16]{0:T(128)S(1)} %bitcast.27, f32[3,64]{1,0:T(4,128)S(1)} %bitcast.16, bf16[16,128,128]{2,1,0:T(8,128)(2,1)S(1)} %get-tuple-element.37.refs_4_, ...), custom_call_target="tpu_custom_call" | custom-call | tf_op jit(solution)/shard_map/match/pallas_call | solution.py:505
  21.4 0.1 plus.3
  21.5 0.7 %collective-permute-start.5 = (bf16[256,512]{1,0:T(8,128)(2,1)S(1)}, bf16[256,512]{1,0:T(8,128)(2,1)S(1)}, u32[]{:S(2)}, u32[]{:S(2)}) collective-permute-start(bf16[256,512]{1,0:T(8,128)(2,1)S(1)} %get-tuple-element.48), channel_id=1, source_target_pairs={{4,8},{8,4},{5,9},{9,5},{6,10},{10,6},{7,11},{11,7},{20,24},{24,20... | collective-permute-start | bytes 786440 | tf_op jit(solution)/shard_map/ppermute | solution.py:554
  22.2 5.7 %collective-permute-start.6 = (bf16[256,512]{1,0:T(8,128)(2,1)S(1)}, bf16[256,512]{1,0:T(8,128)(2,1)S(1)}, u32[]{:S(2)}, u32[]{:S(2)}) collective-permute-start(bf16[256,512]{1,0:T(8,128)(2,1)S(1)} %get-tuple-element.52), channel_id=1, source_target_pairs={{0,4},{4,0},{8,12},{12,8},{1,5},{5,1},{9,13},{13,9},{2,6},{6,2},{1... | collective-permute-start | bytes 786440 | tf_op jit(solution)/shard_map/ppermute | solution.py:553
  27.9 0.3 relay.3
  28.2 0.7 %collective-permute-start.10 = (bf16[256,512]{1,0:T(8,128)(2,1)S(1)}, bf16[256,512]{1,0:T(8,128)(2,1)S(1)}, u32[]{:S(2)}, u32[]{:S(2)}) collective-permute-start(bf16[256,512]{1,0:T(8,128)(2,1)S(1)} %get-tuple-element.61), channel_id=1, source_target_pairs={{4,8},{8,4},{5,9},{9,5},{6,10},{10,6},{7,11},{11,7},{20,24},{24,20... | collective-permute-start | bytes 786440 | tf_op jit(solution)/shard_map/ppermute | solution.py:558
  29.0 3.7 %collective-permute-start.3 = (bf16[256,512]{1,0:T(8,128)(2,1)S(1)}, bf16[256,512]{1,0:T(8,128)(2,1)S(1)}, u32[]{:S(2)}, u32[]{:S(2)}) collective-permute-start(bf16[256,512]{1,0:T(8,128)(2,1)S(1)} %get-tuple-element.44), channel_id=1, source_target_pairs={{0,4},{4,0},{8,12},{12,8},{1,5},{5,1},{9,13},{13,9},{2,6},{6,2},{1... | collective-permute-start | bytes 786440 | tf_op jit(solution)/shard_map/ppermute | solution.py:560
  32.6 0.3 collective-permute-done.6.got
  32.9 0.3 relay.4
  33.2 3.7 %collective-permute-start.8 = (bf16[256,512]{1,0:T(8,128)(2,1)S(1)}, bf16[256,512]{1,0:T(8,128)(2,1)S(1)}, u32[]{:S(2)}, u32[]{:S(2)}) collective-permute-start(bf16[256,512]{1,0:T(8,128)(2,1)S(1)} %get-tuple-element.56), channel_id=1, source_target_pairs={{0,4},{12,8},{1,5},{13,9},{2,6},{14,10},{3,7},{15,11},{16,20},{28,... | collective-permute-start | bytes 786440 | tf_op jit(solution)/shard_map/ppermute | solution.py:565
  36.9 0.7 %collective-permute-start.9 = (bf16[256,512]{1,0:T(8,128)(2,1)S(1)}, bf16[256,512]{1,0:T(8,128)(2,1)S(1)}, u32[]{:S(2)}, u32[]{:S(2)}) collective-permute-start(bf16[256,512]{1,0:T(8,128)(2,1)S(1)} %get-tuple-element.59), channel_id=1, source_target_pairs={{4,8},{8,4},{5,9},{9,5},{6,10},{10,6},{7,11},{11,7},{20,24},{24,20... | collective-permute-start | bytes 786440 | tf_op jit(solution)/shard_map/ppermute | solution.py:564
  37.6 1.8 %collective-permute-done.3.got_d.refs_0_ = bf16[256,512]{1,0:T(8,128)(2,1)S(1)} collective-permute-done((bf16[256,512]{1,0:T(8,128)(2,1)S(1)}, bf16[256,512]{1,0:T(8,128)(2,1)S(1)}, u32[]{:S(2)}, u32[]{:S(2)}) %collective-permute-start.3) | collective-permute-done | bytes 262176 | tf_op jit(solution)/shard_map/ppermute | solution.py:560
  39.4 0.3 relay.5
  39.7 1.3 %collective-permute-start.11 = (bf16[256,512]{1,0:T(8,128)(2,1)S(1)}, bf16[256,512]{1,0:T(8,128)(2,1)S(1)}, u32[]{:S(2)}, u32[]{:S(2)}) collective-permute-start(bf16[256,512]{1,0:T(8,128)(2,1)S(1)} %get-tuple-element.62), channel_id=1, source_target_pairs={{4,0},{8,12},{5,1},{9,13},{6,2},{10,14},{7,3},{11,15},{20,16},{24,... | collective-permute-start | bytes 786440 | tf_op jit(solution)/shard_map/ppermute | solution.py:569
  41.0 2.2 %collective-permute-done.8.got_m = bf16[256,512]{1,0:T(8,128)(2,1)S(1)} collective-permute-done((bf16[256,512]{1,0:T(8,128)(2,1)S(1)}, bf16[256,512]{1,0:T(8,128)(2,1)S(1)}, u32[]{:S(2)}, u32[]{:S(2)}) %collective-permute-start.8) | collective-permute-done | bytes 262176 | tf_op jit(solution)/shard_map/ppermute | solution.py:565
  43.2 0.7 %gather.1 = (f32[256,512]{1,0:T(8,128)S(1)}, f32[256,512]{1,0:T(8,128)S(1)}, f32[256,512]{1,0:T(8,128)S(1)}) custom-call(bf16[256,512]{1,0:T(8,128)(2,1)S(1)} %copy-done.11, bf16[256,512]{1,0:T(8,128)(2,1)S(1)} %copy-done.12, bf16[256,512]{1,0:T(8,128)(2,1)S(1)} %collective-permute-done.3.got_d.refs_0_, ...), custom_call_target="tpu_custom_call" | custom-call | flops 1150000000 | tf_op jit(solution)/shard_map/gather/pallas_call | solution.py:570
  43.9 4.1 %collective-permute-done.11.got_last_m = bf16[256,512]{1,0:T(8,128)(2,1)S(1)} collective-permute-done((bf16[256,512]{1,0:T(8,128)(2,1)S(1)}, bf16[256,512]{1,0:T(8,128)(2,1)S(1)}, u32[]{:S(2)}, u32[]{:S(2)}) %collective-permute-start.11) | collective-permute-done | bytes 262176 | tf_op jit(solution)/shard_map/ppermute | solution.py:569
  48.0 0.3 term.1
  48.4 1.1 %coadd.1 = f32[256,512]{1,0:T(8,128)} custom-call(f32[256,512]{1,0:T(8,128)S(1)} %get-tuple-element.57.matched, f32[256,512]{1,0:T(8,128)S(1)} %get-tuple-element.58.inverse, bf16[256,512]{1,0:T(8,128)(2,1)S(1)} %collective-permute-done.9.got_mid_m, bf16[256,512]{1,0:T(8,128)(2,1)S(1)} %collective-permute-done.11.got_last_m), custom_call_target="tpu_custom_call" | custom-call | flops 1150000000 | tf_op jit(solution)/shard_map/coadd/pallas_call | solution.py:581
  49.5 0.5 collective-permute-done.12
  49.9 0.9 %convert_add_fusion = f32[256,512]{1,0:T(8,128)} fusion(bf16[256,512]{1,0:T(8,128)(2,1)S(1)} %collective-permute-done.12, bf16[256,512]{1,0:T(8,128)(2,1)S(1)} %term.1), kind=kLoop, calls=%fused_computation | loop fusion | flops 393216 | bytes 1048576 | tf_op jit(solution)/shard_map/add | solution.py:594
  (40 shorter events, 0.3 us)
Async XLA Ops:
  0.6 7.5 %copy-start = (bf16[768,256]{1,0:T(8,128)(2,1)S(1)}, bf16[768,256]{1,0:T(8,128)(2,1)}, u32[]{:S(2)}) copy-start(bf16[768,256]{1,0:T(8,128)(2,1)} %constant.8.clone.refs_8_.refs_6_) | copy-start | bytes 1179652
  0.6 7.5 %copy-start.6 = (s32[1,1,16,128,128]{4,3,2,1,0:T(8,128)S(1)}, s32[1,1,16,128,128]{4,3,2,1,0:T(8,128)}, u32[]{:S(2)}) copy-start(s32[1,1,16,128,128]{4,3,2,1,0:T(8,128)} %param.11) | copy-start | bytes 3145732
  0.7 7.5 %copy-start.7 = (bf16[1,1,16,128,128]{4,3,2,1,0:T(8,128)(2,1)S(1)}, bf16[1,1,16,128,128]{4,3,2,1,0:T(8,128)(2,1)}, u32[]{:S(2)}) copy-start(bf16[1,1,16,128,128]{4,3,2,1,0:T(8,128)(2,1)} %param.10) | copy-start | bytes 1572868
  0.7 7.5 %copy-start.9 = (f32[1,1,16]{2,1,0:T(1,128)S(1)}, f32[1,1,16]{2,1,0:T(1,128)}, u32[]{:S(2)}) copy-start(f32[1,1,16]{2,1,0:T(1,128)} %param.12) | copy-start | bytes 196
  0.7 7.5 %copy-start.10 = (bf16[2,96,256]{2,1,0:T(8,128)(2,1)S(1)}, bf16[2,96,256]{2,1,0:T(8,128)(2,1)}, u32[]{:S(2)}) copy-start(bf16[2,96,256]{2,1,0:T(8,128)(2,1)} %constant.9.clone.refs_7_) | copy-start | bytes 294916
  3.2 16.8 %collective-permute-start = (bf16[256,512]{1,0:T(8,128)(2,1)}, bf16[256,512]{1,0:T(8,128)(2,1)S(1)}, u32[]{:S(2)}, u32[]{:S(2)}) collective-permute-start(bf16[256,512]{1,0:T(8,128)(2,1)} %get-tuple-element.35.own), channel_id=1, source_target_pairs={{0,4},{12,8},{1,5},{13,9},{2,6},{14,10},{3,7},{15,11},{16,20},{28,... | collective-permute-start | bytes 786440 | tf_op jit(solution)/shard_map/ppermute | solution.py:472
  8.1 0.7 %copy-start.2 = (f32[64,3]{0,1:T(4,128)S(1)}, f32[64,3]{0,1:T(4,128)}, u32[]{:S(2)}) copy-start(f32[64,3]{0,1:T(4,128)} %param.16) | copy-start | bytes 2308
  8.1 0.7 %copy-start.3 = (s32[1,1,16,1]{2,3,1,0:T(1,128)S(1)}, s32[1,1,16,1]{2,3,1,0:T(1,128)}, u32[]{:S(2)}) copy-start(s32[1,1,16,1]{2,3,1,0:T(1,128)} %param.13) | copy-start | bytes 196
  8.1 0.7 %copy-start.4 = (s32[1,1,16]{2,1,0:T(1,128)S(1)}, s32[1,1,16]{2,1,0:T(1,128)}, u32[]{:S(2)}) copy-start(s32[1,1,16]{2,1,0:T(1,128)} %param.14) | copy-start | bytes 196
  8.1 0.7 %copy-start.5 = (s32[1,1,16]{2,1,0:T(1,128)S(1)}, s32[1,1,16]{2,1,0:T(1,128)}, u32[]{:S(2)}) copy-start(s32[1,1,16]{2,1,0:T(1,128)} %param.15) | copy-start | bytes 196
  8.8 0.9 %copy-start.13 = (bf16[256,512]{1,0:T(8,128)(2,1)S(1)}, bf16[256,512]{1,0:T(8,128)(2,1)}, u32[]{:S(2)}) copy-start(bf16[256,512]{1,0:T(8,128)(2,1)} %get-tuple-element.36.refs_9_) | copy-start | bytes 786436
  9.8 5.5 %copy-start.1 = (bf16[528,256]{1,0:T(8,128)(2,1)S(1)}, bf16[528,256]{1,0:T(8,128)(2,1)}, u32[]{:S(2)}) copy-start(bf16[528,256]{1,0:T(8,128)(2,1)} %constant.10.clone.refs_5_) | copy-start | bytes 811012
  12.4 6.0 %collective-permute-start.1 = (bf16[4,32,512]{2,1,0:T(8,128)(2,1)S(1)}, bf16[4,32,512]{2,1,0:T(8,128)(2,1)S(1)}, u32[]{:S(2)}, u32[]{:S(2)}) collective-permute-start(bf16[4,32,512]{2,1,0:T(8,128)(2,1)S(1)} %get-tuple-element.41), channel_id=1, source_target_pairs={{0,2},{2,0},{1,3},{3,1},{4,6},{6,4},{5,7},{7,5},{8,10},{10,8},{9,1... | collective-permute-start | bytes 393224 | tf_op jit(solution)/shard_map/ppermute | solution.py:500
  14.0 7.4 %collective-permute-start.4 = (bf16[256,512]{1,0:T(8,128)(2,1)S(1)}, bf16[256,512]{1,0:T(8,128)(2,1)S(1)}, u32[]{:S(2)}, u32[]{:S(2)}) collective-permute-start(bf16[256,512]{1,0:T(8,128)(2,1)S(1)} %get-tuple-element.45.own), channel_id=1, source_target_pairs={{0,4},{12,8},{1,5},{13,9},{2,6},{14,10},{3,7},{15,11},{16,20},{28,... | collective-permute-start | bytes 786440 | tf_op jit(solution)/shard_map/ppermute | solution.py:501
  18.5 1.5 %copy-start.8 = (bf16[256,512]{1,0:T(8,128)(2,1)S(1)}, bf16[256,512]{1,0:T(8,128)(2,1)}, u32[]{:S(2)}) copy-start(bf16[256,512]{1,0:T(8,128)(2,1)} %get-tuple-element.35.own) | copy-start | bytes 786436
  18.7 9.2 %collective-permute-start.7 = (bf16[256,512]{1,0:T(8,128)(2,1)S(1)}, bf16[256,512]{1,0:T(8,128)(2,1)S(1)}, u32[]{:S(2)}, u32[]{:S(2)}) collective-permute-start(bf16[256,512]{1,0:T(8,128)(2,1)S(1)} %get-tuple-element.53), channel_id=1, source_target_pairs={{0,4},{12,8},{1,5},{13,9},{2,6},{14,10},{3,7},{15,11},{16,20},{28,... | collective-permute-start | bytes 786440 | tf_op jit(solution)/shard_map/ppermute | solution.py:540
  20.1 7.8 %collective-permute-start.2 = (bf16[256,512]{1,0:T(8,128)(2,1)S(1)}, bf16[256,512]{1,0:T(8,128)(2,1)S(1)}, u32[]{:S(2)}, u32[]{:S(2)}) collective-permute-start(bf16[256,512]{1,0:T(8,128)(2,1)S(1)} %get-tuple-element.43.refs_7_), channel_id=1, source_target_pairs={{4,8},{8,4},{5,9},{9,5},{6,10},{10,6},{7,11},{11,7},{20,24},{24,20... | collective-permute-start | bytes 786440 | tf_op jit(solution)/shard_map/ppermute | solution.py:542
  21.5 16.1 %collective-permute-start.5 = (bf16[256,512]{1,0:T(8,128)(2,1)S(1)}, bf16[256,512]{1,0:T(8,128)(2,1)S(1)}, u32[]{:S(2)}, u32[]{:S(2)}) collective-permute-start(bf16[256,512]{1,0:T(8,128)(2,1)S(1)} %get-tuple-element.48), channel_id=1, source_target_pairs={{4,8},{8,4},{5,9},{9,5},{6,10},{10,6},{7,11},{11,7},{20,24},{24,20... | collective-permute-start | bytes 786440 | tf_op jit(solution)/shard_map/ppermute | solution.py:554
  22.2 10.8 %collective-permute-start.6 = (bf16[256,512]{1,0:T(8,128)(2,1)S(1)}, bf16[256,512]{1,0:T(8,128)(2,1)S(1)}, u32[]{:S(2)}, u32[]{:S(2)}) collective-permute-start(bf16[256,512]{1,0:T(8,128)(2,1)S(1)} %get-tuple-element.52), channel_id=1, source_target_pairs={{0,4},{4,0},{8,12},{12,8},{1,5},{5,1},{9,13},{13,9},{2,6},{6,2},{1... | collective-permute-start | bytes 786440 | tf_op jit(solution)/shard_map/ppermute | solution.py:553
  27.9 1.0 %copy-start.11 = (bf16[256,512]{1,0:T(8,128)(2,1)S(1)}, bf16[256,512]{1,0:T(8,128)(2,1)}, u32[]{:S(2)}) copy-start(bf16[256,512]{1,0:T(8,128)(2,1)} %get-tuple-element.33.third.third_d) | copy-start | bytes 786436
  27.9 1.0 %copy-start.12 = (bf16[256,512]{1,0:T(8,128)(2,1)S(1)}, bf16[256,512]{1,0:T(8,128)(2,1)}, u32[]{:S(2)}) copy-start(bf16[256,512]{1,0:T(8,128)(2,1)} %get-tuple-element.34.last.last_d) | copy-start | bytes 786436
  28.2 9.4 %collective-permute-start.10 = (bf16[256,512]{1,0:T(8,128)(2,1)S(1)}, bf16[256,512]{1,0:T(8,128)(2,1)S(1)}, u32[]{:S(2)}, u32[]{:S(2)}) collective-permute-start(bf16[256,512]{1,0:T(8,128)(2,1)S(1)} %get-tuple-element.61), channel_id=1, source_target_pairs={{4,8},{8,4},{5,9},{9,5},{6,10},{10,6},{7,11},{11,7},{20,24},{24,20... | collective-permute-start | bytes 786440 | tf_op jit(solution)/shard_map/ppermute | solution.py:558
  29.0 10.4 %collective-permute-start.3 = (bf16[256,512]{1,0:T(8,128)(2,1)S(1)}, bf16[256,512]{1,0:T(8,128)(2,1)S(1)}, u32[]{:S(2)}, u32[]{:S(2)}) collective-permute-start(bf16[256,512]{1,0:T(8,128)(2,1)S(1)} %get-tuple-element.44), channel_id=1, source_target_pairs={{0,4},{4,0},{8,12},{12,8},{1,5},{5,1},{9,13},{13,9},{2,6},{6,2},{1... | collective-permute-start | bytes 786440 | tf_op jit(solution)/shard_map/ppermute | solution.py:560
  33.2 10.0 %collective-permute-start.8 = (bf16[256,512]{1,0:T(8,128)(2,1)S(1)}, bf16[256,512]{1,0:T(8,128)(2,1)S(1)}, u32[]{:S(2)}, u32[]{:S(2)}) collective-permute-start(bf16[256,512]{1,0:T(8,128)(2,1)S(1)} %get-tuple-element.56), channel_id=1, source_target_pairs={{0,4},{12,8},{1,5},{13,9},{2,6},{14,10},{3,7},{15,11},{16,20},{28,... | collective-permute-start | bytes 786440 | tf_op jit(solution)/shard_map/ppermute | solution.py:565
  36.9 7.0 %collective-permute-start.9 = (bf16[256,512]{1,0:T(8,128)(2,1)S(1)}, bf16[256,512]{1,0:T(8,128)(2,1)S(1)}, u32[]{:S(2)}, u32[]{:S(2)}) collective-permute-start(bf16[256,512]{1,0:T(8,128)(2,1)S(1)} %get-tuple-element.59), channel_id=1, source_target_pairs={{4,8},{8,4},{5,9},{9,5},{6,10},{10,6},{7,11},{11,7},{20,24},{24,20... | collective-permute-start | bytes 786440 | tf_op jit(solution)/shard_map/ppermute | solution.py:564
  39.7 8.3 %collective-permute-start.11 = (bf16[256,512]{1,0:T(8,128)(2,1)S(1)}, bf16[256,512]{1,0:T(8,128)(2,1)S(1)}, u32[]{:S(2)}, u32[]{:S(2)}) collective-permute-start(bf16[256,512]{1,0:T(8,128)(2,1)S(1)} %get-tuple-element.62), channel_id=1, source_target_pairs={{4,0},{8,12},{5,1},{9,13},{6,2},{10,14},{7,3},{11,15},{20,16},{24,... | collective-permute-start | bytes 786440 | tf_op jit(solution)/shard_map/ppermute | solution.py:569
  48.3 1.6 %collective-permute-start.12 = (bf16[256,512]{1,0:T(8,128)(2,1)S(1)}, bf16[256,512]{1,0:T(8,128)(2,1)S(1)}, u32[]{:S(2)}, u32[]{:S(2)}) collective-permute-start(bf16[256,512]{1,0:T(8,128)(2,1)S(1)} %term.1), channel_id=1, source_target_pairs={{0,1},{1,0},{2,3},{3,2},{4,5},{5,4},{6,7},{7,6},{8,9},{9,8},{10,11... | collective-permute-start | bytes 786440 | tf_op jit(solution)/shard_map/ppermute | solution.py:593
